TPU v7x, 32 devices: a whole 2x2x4 slice. The times are simulated.
32 devices in a mesh: groups: 2 (over x), band: 8 (over z, y), sub: 2 (over core).
Axes of the slice: x: 2, y: 2, z: 4, core: 2. Of those that a mesh axis runs over, the one named last changes fastest.
Arguments:
- state: bfloat16 [154, 96, 240], P('groups', 'band', 'sub'), parts along dimension 0, may hold values from -6 to 6
- target: bfloat16 [154, 96, 240], P('groups', 'band', 'sub'), parts along dimension 0, may hold values from -6 to 6
- tile_plan: int32 [16, 20], P('groups'), parts along dimension 0, may hold values from -1 to 31, as said below
- w_enc: bfloat16 [77, 256], replicated, may hold values from -0.625 to 0.625
- dw_kernel: bfloat16 [49, 256], replicated, may hold values from -0.875 to 0.875
- norm_gain: float32 [256], replicated, may hold values from 0.1 to 1.9
- w_up: bfloat16 [256, 1024], replicated, may hold values from -0.375 to 0.375
- w_down: bfloat16 [1024, 256], replicated, may hold values from -0.1875 to 0.1875
- w_dec: bfloat16 [256, 77], replicated, may hold values from -0.375 to 0.375
Outputs:
- predicted_state: bfloat16 [154, 96, 240], P('groups', 'band', 'sub'), parts along dimension 0
- loss: float32 [2], P('groups'), parts along dimension 0
- grad_w_enc: float32 [154, 256], P('groups'), parts along dimension 0
- grad_dw_kernel: float32 [98, 256], P('groups'), parts along dimension 0
- grad_norm_gain: float32 [512], P('groups'), parts along dimension 0
- grad_w_up: float32 [512, 1024], P('groups'), parts along dimension 0
- grad_w_down: float32 [2048, 256], P('groups'), parts along dimension 0
- grad_w_dec: float32 [512, 77], P('groups'), parts along dimension 0
There are 2 independent parts, one for each index of `groups`. A program takes and returns all parts, laid end to end along the dimension named above; an argument that names none is the same for every part. Nothing has to cross between parts.
Inputs may be any that keep to these rules, and one draw needn't show every extreme that they name: `tile_plan`: for a wet tile held by band index e in one half of sub, the value d * 4 + s names band index d and slot s of a computing device in the same half of sub, where d - e taken cyclically over the band indices lies between -2 and 2. In each half of sub every slot of every band index is named by exactly one wet tile. Wet tiles come in pairs of longitude neighbours (tile columns 2m and 2m+1 of one device's 10 columns) that go to one device in slots 2k and 2k+1, and one device holds at most one such pair for one computing band, so at most 2 tiles; every draw reaches that.
All inputs are finite; a program needn't handle non-finite values.
Results may differ from a plain program's by a relative error of at most 0.0042.
Values may be sent and summed in bfloat16 or wider, within the bound.
A program may use at most 64 MiB of HBM per device.

v0:
```python
import functools
import math

import jax
import jax.numpy as jnp
from jax import lax
from jax.experimental import pallas as pl
from jax.experimental.pallas import tpu as pltpu
from jax.sharding import PartitionSpec as P

KSIZE = 7
RIM = 3
PW = 12
LANES = 128
F32 = jnp.float32
BF16 = jnp.bfloat16
GELU_C = math.sqrt(2.0 / math.pi)
GELU_A = 0.044715


def with_halo(value, axis, dim, width, wrap):
    size, length = (lax.axis_size(axis), value.shape[dim])
    up = [(i, (i + 1) % size) for i in range(size if wrap else size - 1)]
    down = [(j, i) for i, j in up]
    last = lax.slice_in_dim(value, length - width, length, axis=dim)
    leading = lax.slice_in_dim(value, 0, width, axis=dim)
    return lax.ppermute(last, axis, up), lax.ppermute(leading, axis, down)


def dot(left, right, dims):
    return lax.dot_general(left, right, ((dims[:1], dims[1:]), ((), ())), preferred_element_type=F32)


def block_kernel(
    x_ref, goal_ref, mask_ref, gscale_ref, w_enc_ref, dw_ref, gain_ref, w_up_ref, w_down_ref,
    w_dec_t_ref, pred_ref, pack_ref, shifted, conv, gres_all, taps, dk, up_acc, down_acc,
):
    chan = x_ref.shape[1]
    width = w_enc_ref.shape[1]
    hid = w_up_ref.shape[1]
    rows = goal_ref.shape[0]
    wide = rows + KSIZE - 1
    groups = (LANES - 8) // 8
    lane_parts = width // LANES
    base_down = hid
    base_enc = 2 * hid
    base_dec = base_enc + 80
    base_dw = base_dec + 80
    base_small = base_dw + 56

    for i in range(KSIZE * KSIZE):
        taps[i] = jnp.broadcast_to(dw_ref[i : i + 1, :], (8, width))
    dk[...] = jnp.zeros_like(dk)
    up_acc[...] = jnp.zeros_like(up_acc)
    down_acc[...] = jnp.zeros_like(down_acc)
    gres_all[...] = jnp.zeros_like(gres_all)
    pack_ref[base_enc:, :] = jnp.zeros((pack_ref.shape[0] - base_enc, width), F32)
    inside = lax.broadcasted_iota(jnp.int32, (LANES, width), 0) < groups * 8

    @pl.loop(0, wide)
    def _(r):
        enc = dot(x_ref[r], w_enc_ref[...], (0, 0)).astype(BF16).astype(F32)
        for b in range(KSIZE):
            moved = enc if b == 0 else pltpu.roll(enc, LANES - b, 0)
            shifted[b, r] = jnp.where(inside, moved, 0.0)

    conv[:, groups * 8 :, :] = jnp.zeros((rows, LANES - groups * 8, width), F32)

    @pl.loop(0, groups * lane_parts)
    def _(step):
        at = (
            pl.ds(pl.multiple_of((step // lane_parts) * 8, 8), 8),
            pl.ds(pl.multiple_of((step % lane_parts) * LANES, LANES), LANES),
        )
        acc = [None] * rows
        for b in range(KSIZE):
            line = [shifted[(b, r) + at] for r in range(wide)]
            for a in range(KSIZE):
                tap = taps[a * KSIZE + b, :, at[1]]
                for y in range(rows):
                    term = line[y + a] * tap
                    acc[y] = term if acc[y] is None else acc[y] + term
        for y in range(rows):
            conv[(y,) + at] = acc[y]

    gain = gain_ref[...]
    mask = jnp.concatenate([mask_ref[...]] * 2, axis=1)
    gscale = jnp.concatenate([gscale_ref[...]] * 2, axis=1)

    @pl.loop(0, rows // 2)
    def _(step):
        y = step * 2
        cv = conv[pl.ds(y, 2)].reshape(2 * LANES, width)
        centred = cv - jnp.mean(cv, axis=-1, keepdims=True)
        inv_std = lax.rsqrt(jnp.mean(centred * centred, axis=-1, keepdims=True) + 1e-06)
        normed = centred * inv_std
        scaled = (normed * gain).astype(BF16)
        pre = dot(scaled, w_up_ref[...], (1, 0))
        square = pre * pre
        th = jnp.tanh(GELU_C * (pre + GELU_A * (square * pre)))
        half = 0.5 * (1.0 + th)
        act = (pre * half).astype(BF16)
        slope = half + (0.5 * GELU_C) * pre * (1.0 - th * th) * (1.0 + (3.0 * GELU_A) * square)
        centre = shifted[RIM, pl.ds(y + RIM, 2)].reshape(2 * LANES, width)
        residual = (centre + dot(act, w_down_ref[...], (1, 0))).astype(BF16)
        readout = dot(w_dec_t_ref[...], residual, (1, 1))
        base = jnp.concatenate(
            [
                pltpu.roll(x_ref[y + RIM + i].astype(F32), LANES - RIM, 1)
                for i in range(2)
            ],
            axis=1,
        )
        goal = jnp.concatenate([goal_ref[y + i] for i in range(2)], axis=1).astype(F32)
        pred = base + readout
        keep = jnp.where(mask > 0.0, pred, base).astype(BF16)
        pred_ref[y] = keep[:, :LANES]
        pred_ref[y + 1] = keep[:, LANES:]
        misfit = (pred - goal) * mask
        pack_ref[base_small : base_small + 1, :] += jnp.sum(misfit * misfit, axis=0, keepdims=True)
        gout = (misfit * gscale).astype(BF16)
        pack_ref[base_dec : base_dec + chan, :] += dot(gout, residual, (1, 0))
        gres = dot(gout, w_dec_t_ref[...], (0, 0)).astype(BF16)
        gres_all[pl.ds(y + RIM, 2)] = gres.astype(F32).reshape(2, LANES, width)
        down_acc[...] += dot(gres, act, (0, 0))
        gpre = (dot(gres, w_down_ref[...], (1, 1)) * slope).astype(BF16)
        up_acc[...] += dot(scaled, gpre, (0, 0))
        gscaled = dot(gpre, w_up_ref[...], (1, 1))
        pack_ref[base_small + 1 : base_small + 2, :] += jnp.sum(
            gscaled * normed, axis=0, keepdims=True
        )
        g = gscaled * gain
        gconv = inv_std * (
            g
            - jnp.mean(g, axis=-1, keepdims=True)
            - normed * jnp.mean(g * normed, axis=-1, keepdims=True)
        )
        conv[pl.ds(y, 2)] = gconv.reshape(2, LANES, width)

    @pl.loop(0, groups * lane_parts)
    def _(step):
        at = (
            pl.ds(pl.multiple_of((step // lane_parts) * 8, 8), 8),
            pl.ds(pl.multiple_of((step % lane_parts) * LANES, LANES), LANES),
        )
        gc = [conv[(y,) + at] for y in range(rows)]
        for b in range(KSIZE):
            line = [shifted[(b, r) + at] for r in range(wide)]
            for a in range(KSIZE):
                total = gc[0] * line[a]
                for y in range(1, rows):
                    total = total + gc[y] * line[y + a]
                dk[a * KSIZE + b, :, at[1]] += total
            spread = [None] * wide
            for a in range(KSIZE):
                tap = taps[a * KSIZE + b, :, at[1]]
                for y in range(rows):
                    term = gc[y] * tap
                    old = spread[y + a]
                    spread[y + a] = term if old is None else old + term
            for r in range(wide):
                shifted[(b, r) + at] = spread[r]

    @pl.loop(0, wide)
    def _(r):
        g = pltpu.roll(gres_all[r], RIM, 0) + shifted[0, r]
        for b in range(1, KSIZE):
            g = g + pltpu.roll(shifted[b, r], b, 0)
        pack_ref[base_enc : base_enc + chan, :] += dot(x_ref[r], g.astype(BF16), (1, 0))

    for i in range(KSIZE * KSIZE):
        pack_ref[base_dw + i : base_dw + i + 1, :] = jnp.sum(dk[i], axis=0, keepdims=True)
    for k in range(hid // width):
        cols = slice(k * width, (k + 1) * width)
        pack_ref[cols, :] = up_acc[:, cols]
        pack_ref[base_down + k * width : base_down + (k + 1) * width, :] = down_acc[:, cols].T


def shards(state, target, tile_plan, w_enc, dw_kernel, norm_gain, w_up, w_down, w_dec):
    chan, rows, cols = state.shape
    width, hid = w_up.shape
    wide = rows + KSIZE - 1
    tile_cols = cols // PW
    band_at = lax.axis_index("band")
    sub_at = lax.axis_index("sub")
    before, after = with_halo(state, "sub", 2, RIM, True)
    fill = jnp.zeros((chan, rows, LANES - cols - 2 * RIM), BF16)
    lon = jnp.concatenate([before, state, after, fill], axis=2)
    above, below = with_halo(lon, "band", 1, RIM, False)
    x = jnp.concatenate([above, lon, below], axis=1).transpose(1, 0, 2)
    goal = jnp.pad(target.transpose(1, 0, 2), ((0, 0), (0, 0), (0, LANES - cols)))
    plan = lax.dynamic_slice(tile_plan, (band_at, sub_at * tile_cols), (1, tile_cols))
    wet = (plan >= 0).astype(F32)
    mask = jnp.pad(jnp.repeat(wet, PW, axis=1), ((0, 0), (0, LANES - cols)))
    inv_count = 1.0 / (jnp.sum((tile_plan >= 0).astype(F32)) * (chan * PW * PW))
    pack_rows = 2 * hid + 80 + 80 + 56 + 8
    vmem = pl.BlockSpec(memory_space=pltpu.VMEM)
    pred, pack = pl.pallas_call(
        block_kernel,
        out_shape=(
            jax.ShapeDtypeStruct((rows, chan, LANES), BF16),
            jax.ShapeDtypeStruct((pack_rows, width), F32),
        ),
        in_specs=[vmem] * 10,
        out_specs=(vmem, vmem),
        scratch_shapes=[
            pltpu.VMEM((KSIZE, wide, LANES, width), F32),
            pltpu.VMEM((rows, LANES, width), F32),
            pltpu.VMEM((wide, LANES, width), F32),
            pltpu.VMEM((KSIZE * KSIZE, 8, width), F32),
            pltpu.VMEM((KSIZE * KSIZE, 8, width), F32),
            pltpu.VMEM((width, hid), F32),
            pltpu.VMEM((width, hid), F32),
        ],
        compiler_params=pltpu.CompilerParams(vmem_limit_bytes=52 * 1024 * 1024),
        name="block",
    )(
        x, goal, mask, mask * (2.0 * inv_count), w_enc, dw_kernel.astype(F32),
        norm_gain.reshape(1, width), w_up, w_down, w_dec.T,
    )
    new_field = pred[:, :, :cols].transpose(1, 0, 2)
    total = lax.psum(pack, ("band", "sub"))
    g_up = jnp.concatenate([total[k * width : (k + 1) * width] for k in range(hid // width)], axis=1)
    at = 2 * hid
    return (
        new_field,
        (jnp.sum(total[at + 216]) * inv_count).reshape(1),
        total[at : at + chan],
        total[at + 160 : at + 160 + KSIZE * KSIZE],
        total[at + 217],
        g_up,
        total[hid : 2 * hid],
        total[at + 80 : at + 80 + chan].T,
    )


def solution(mesh):
    split = P("groups", "band", "sub")
    parts = P("groups", None)
    return jax.shard_map(
        shards,
        mesh=mesh,
        in_specs=(split, split, parts) + (P(),) * 6,
        out_specs=(split, P("groups"), parts, parts, P("groups"), parts, parts, parts),
        check_vma=False,
    )
```

profile of v0, /device:TPU:0, one launch (start us, length us, event | category | flops | bytes accessed | tf_op | source)
XLA Modules:
  0.0 184.5 jit_solution(6701352690301615383)
XLA Ops:
  7.2 0.0 copy-start.4
  7.2 0.0 all-reduce.4.cloned.1.call-start
  7.3 1.3 fusion.3
  8.6 0.5 collective-permute-start
  9.1 0.1 collective-permute-start.1
  9.2 1.3 convert_reduce_fusion
  10.5 0.8 fusion
  11.2 0.1 broadcast_in_dim.9
  11.3 0.1 broadcast_in_dim.10
  11.4 0.8 convert_element_type.18.dw_ref
  12.8 1.0 pad.8.goal_ref
  13.8 0.0 collective-permute-done
  13.8 0.0 collective-permute-done.1
  13.9 1.0 pad_maximum_fusion.4
  14.9 4.9 %collective-permute-start.2 = (bf16[77,3,128]{2,0,1:T(8,128)(2,1)S(1)}, bf16[77,3,128]{2,0,1:T(8,128)(2,1)S(1)}, u32[]{:S(2)}, u32[]{:S(2)}) collective-permute-start(bf16[77,3,128]{2,0,1:T(8,128)(2,1)S(1)} %get-tuple-element.20), channel_id=1, source_target_pairs={{0,2},{2,4},{4,6},{6,8},{8,10},{10,12},{12,14},{1,3},{3,5},{5,7},{... | collective-permute-start | bytes 177416 | tf_op jit(solution)/shard_map/ppermute | solution.py:27
  19.8 1.3 collective-permute-start.3
  21.1 0.5 collective-permute-done.2
  21.6 4.3 %collective-permute-done.3 = bf16[77,3,128]{2,0,1:T(8,128)(2,1)S(1)} collective-permute-done((bf16[77,3,128]{2,0,1:T(8,128)(2,1)S(1)}, bf16[77,3,128]{2,0,1:T(8,128)(2,1)S(1)}, u32[]{:S(2)}, u32[]{:S(2)}) %collective-permute-start.3) | collective-permute-done | bytes 59168 | tf_op jit(solution)/shard_map/ppermute | solution.py:27
  25.9 0.3 maximum_bitcast_fusion.x_ref
  26.3 0.0 copy-done.2
  26.3 0.0 copy-done
  26.3 0.0 copy-done.3
  26.3 42.7 %block.1 = (bf16[12,77,128]{2,1,0:T(8,128)(2,1)S(1)}, f32[2272,256]{1,0:T(8,128)}) custom-call(bf16[18,77,128]{2,1,0:T(8,128)(2,1)S(1)} %maximum_bitcast_fusion.x_ref, bf16[12,77,128]{2,1,0:T(8,128)(2,1)S(1)} %pad.8.goal_ref, f32[1,128]{1,0:T(1,128)S(1)} %get-tuple-element.25.mask_ref, f32[1,128]{1,0:T(1,128)S(1)} %get-tuple-element.24.gscale_ref, ...), custom_call_target="tpu_custom_call" | custom-call | tf_op jit(solution)/shard_map/block/pallas_call | solution.py:198
  69.0 0.0 all-reduce.4.cloned.1.call-update
  69.0 0.7 slice_bitcast_fusion
  69.7 99.4 %all-reduce.4.cloned.1.call-done = f32[2272,256]{1,0:T(8,128)} async-done(((f32[2272,256]{1,0:T(8,128)}), f32[2272,256]{1,0:T(8,128)}) %all-reduce.4.cloned.1.call-update) | async-done | bytes 2326544 | tf_op jit(solution)/shard_map/psum | solution.py:222
  169.2 2.0 %fusion.2 = (f32[1,256]{1,0:T(1,128)}, f32[]{:T(128)}) fusion(f32[2272,256]{1,0:T(8,128)} %all-reduce.4.cloned.1.call-done), kind=kLoop, calls=%fused_computation.14 | loop fusion | flops 255 | bytes 3076 | tf_op jit(solution)/shard_map/slice | solution.py:230
  171.8 1.3 fusion.1
  173.1 1.1 pad_maximum_fusion
  174.2 0.6 slice.62
  174.8 0.7 slice_bitcast_fusion.1
  175.5 1.0 slice.68
  (10 shorter events, 0.1 us)
Async XLA Ops:
  7.2 18.7 %copy-start.4 = (bf16[77,12,120]{2,0,1:T(8,128)(2,1)S(1)}, bf16[77,12,120]{2,0,1:T(8,128)(2,1)}, u32[]{:S(2)}) copy-start(bf16[77,12,120]{2,0,1:T(8,128)(2,1)} %param.9) | copy-start | bytes 665284
  7.2 19.1 %copy-start.2 = (bf16[256,77]{0,1:T(8,128)(2,1)S(1)}, bf16[256,77]{0,1:T(8,128)(2,1)}, u32[]{:S(2)}) copy-start(bf16[256,77]{0,1:T(8,128)(2,1)} %param.17) | copy-start | bytes 118276
  7.2 19.1 %copy-start = (bf16[256,1024]{1,0:T(8,128)(2,1)S(1)}, bf16[256,1024]{1,0:T(8,128)(2,1)}, u32[]{:S(2)}) copy-start(bf16[256,1024]{1,0:T(8,128)(2,1)} %w_up_ref.1) | copy-start | bytes 1572868
  7.2 19.1 %copy-start.3 = (f32[256]{0:T(256)S(1)}, f32[256]{0:T(256)}, u32[]{:S(2)}) copy-start(f32[256]{0:T(256)} %param.14) | copy-start | bytes 3076
  7.2 19.1 %copy-start.1 = (bf16[77,256]{1,0:T(8,128)(2,1)S(1)}, bf16[77,256]{1,0:T(8,128)(2,1)}, u32[]{:S(2)}) copy-start(bf16[77,256]{1,0:T(8,128)(2,1)} %w_enc_ref.1) | copy-start | bytes 118276
  7.2 161.9 %all-reduce.4.cloned.1.call-start = ((), (), s32[]{:S(2)}) async-start(), calls=%async_computation | async-start | bytes 4653056 | tf_op jit(solution)/shard_map/psum | solution.py:222
  8.6 5.3 %collective-permute-start = (bf16[77,12,3]{2,0,1:T(8,128)(2,1)S(1)}, bf16[77,12,3]{2,0,1:T(8,128)(2,1)S(1)}, u32[]{:S(2)}, u32[]{:S(2)}) collective-permute-start(bf16[77,12,3]{2,0,1:T(8,128)(2,1)S(1)} %get-tuple-element.22), channel_id=1, source_target_pairs={{0,1},{1,0},{2,3},{3,2},{4,5},{5,4},{6,7},{7,6},{8,9},{9,8},{10,11... | collective-permute-start | bytes 16640 | tf_op jit(solution)/shard_map/ppermute | solution.py:27
  9.1 4.8 %collective-permute-start.1 = (bf16[77,12,3]{2,0,1:T(8,128)(2,1)S(1)}, bf16[77,12,3]{2,0,1:T(8,128)(2,1)S(1)}, u32[]{:S(2)}, u32[]{:S(2)}) collective-permute-start(bf16[77,12,3]{2,0,1:T(8,128)(2,1)S(1)} %get-tuple-element.23), channel_id=1, source_target_pairs={{1,0},{0,1},{3,2},{2,3},{5,4},{4,5},{7,6},{6,7},{9,8},{8,9},{11,10... | collective-permute-start | bytes 16640 | tf_op jit(solution)/shard_map/ppermute | solution.py:27
  14.9 6.7 %collective-permute-start.2 = (bf16[77,3,128]{2,0,1:T(8,128)(2,1)S(1)}, bf16[77,3,128]{2,0,1:T(8,128)(2,1)S(1)}, u32[]{:S(2)}, u32[]{:S(2)}) collective-permute-start(bf16[77,3,128]{2,0,1:T(8,128)(2,1)S(1)} %get-tuple-element.20), channel_id=1, source_target_pairs={{0,2},{2,4},{4,6},{6,8},{8,10},{10,12},{12,14},{1,3},{3,5},{5,7},{... | collective-permute-start | bytes 177416 | tf_op jit(solution)/shard_map/ppermute | solution.py:27
  19.8 6.1 %collective-permute-start.3 = (bf16[77,3,128]{2,0,1:T(8,128)(2,1)S(1)}, bf16[77,3,128]{2,0,1:T(8,128)(2,1)S(1)}, u32[]{:S(2)}, u32[]{:S(2)}) collective-permute-start(bf16[77,3,128]{2,0,1:T(8,128)(2,1)S(1)} %get-tuple-element.21), channel_id=1, source_target_pairs={{2,0},{4,2},{6,4},{8,6},{10,8},{12,10},{14,12},{3,1},{5,3},{7,5},{... | collective-permute-start | bytes 177416 | tf_op jit(solution)/shard_map/ppermute | solution.py:27
  169.2 5.0 %copy-start.5 = (f32[2272,256]{1,0:T(8,128)S(1)}, f32[2272,256]{1,0:T(8,128)}, u32[]{:S(2)}) copy-start(f32[2272,256]{1,0:T(8,128)} %all-reduce.4.cloned.1.call-done) | copy-start | bytes 6979588
Sparse Core Ops, SparseCore 0:
  69.1 99.9 all-reduce.3
where the time goes:
time: 185 us
  waiting for transfers between devices  104 us (56%)
  Pallas kernels  42.7 us (23%)
  between operations  16.7 us (9%)
  other arithmetic  7.33 us (4%)
  local copies, waits for them, and re-layouts  6.82 us (4%)
  starting transfers between devices  6.78 us (4%)
    psum x1, waiting for transfers between devices, shards(): total = lax.psum(pack, ('band', 'sub'))  99.4 us
    pallas_call x1, Pallas kernels, shards(): pl.pallas_call(block_kernel, out_shape=(jax.ShapeDtypeStruct((rows, chan,...  42.7 us
    ppermute x4, starting transfers between devices, with_halo(): return (lax.ppermute(last, axis, up), lax.ppermute(leading, axis, down))  6.74 us
    ppermute x4, waiting for transfers between devices, with_halo(): return (lax.ppermute(last, axis, up), lax.ppermute(leading, axis, down))  4.8 us
  transfers between devices with their start and end apart: 5, of which 3 were waited for; matrix products, arithmetic and copies ran while one was open for 3% of the time, Pallas kernels for 0%

commit v1 on v0

--- a/solution.py
+++ b/solution.py
@@ -33,7 +33,7 @@
 
 def block_kernel(
     x_ref, goal_ref, mask_ref, gscale_ref, w_enc_ref, dw_ref, gain_ref, w_up_ref, w_down_ref,
-    w_dec_t_ref, pred_ref, pack_ref, shifted, conv, gres_all, taps, dk, up_acc, down_acc,
+    w_dec_t_ref, pred_ref, pack_ref, small_ref, shifted, conv, gres_all, taps, dk, up_acc, down_acc,
 ):
     chan = x_ref.shape[1]
     width = w_enc_ref.shape[1]
@@ -46,7 +46,6 @@
     base_enc = 2 * hid
     base_dec = base_enc + 80
     base_dw = base_dec + 80
-    base_small = base_dw + 56
 
     for i in range(KSIZE * KSIZE):
         taps[i] = jnp.broadcast_to(dw_ref[i : i + 1, :], (8, width))
@@ -55,6 +54,7 @@
     down_acc[...] = jnp.zeros_like(down_acc)
     gres_all[...] = jnp.zeros_like(gres_all)
     pack_ref[base_enc:, :] = jnp.zeros((pack_ref.shape[0] - base_enc, width), F32)
+    small_ref[...] = jnp.zeros_like(small_ref)
     inside = lax.broadcasted_iota(jnp.int32, (LANES, width), 0) < groups * 8
 
     @pl.loop(0, wide)
@@ -117,7 +117,7 @@
         pred_ref[y] = keep[:, :LANES]
         pred_ref[y + 1] = keep[:, LANES:]
         misfit = (pred - goal) * mask
-        pack_ref[base_small : base_small + 1, :] += jnp.sum(misfit * misfit, axis=0, keepdims=True)
+        small_ref[0:1, :] += jnp.sum(misfit * misfit, axis=0, keepdims=True)
         gout = (misfit * gscale).astype(BF16)
         pack_ref[base_dec : base_dec + chan, :] += dot(gout, residual, (1, 0))
         gres = dot(gout, w_dec_t_ref[...], (0, 0)).astype(BF16)
@@ -126,7 +126,7 @@
         gpre = (dot(gres, w_down_ref[...], (1, 1)) * slope).astype(BF16)
         up_acc[...] += dot(scaled, gpre, (0, 0))
         gscaled = dot(gpre, w_up_ref[...], (1, 1))
-        pack_ref[base_small + 1 : base_small + 2, :] += jnp.sum(
+        small_ref[1:2, :] += jnp.sum(
             gscaled * normed, axis=0, keepdims=True
         )
         g = gscaled * gain
@@ -176,6 +176,189 @@
         pack_ref[base_down + k * width : base_down + (k + 1) * width, :] = down_acc[:, cols].T
 
 
+def sum_kernel(
+    ranges, band_size, pack_ref, small_ref, up_ref, down_ref, enc_ref, dw_ref, dec_ref, small_out,
+    acc, core_in, out_buf, in_buf, res, small_now, small_in, send_sem, recv_sem, small_send, small_recv,
+):
+    band = lax.axis_index("band")
+    sub = lax.axis_index("sub")
+    bits = band_size.bit_length() - 1
+    core = {"band": band, "sub": 1 - sub}
+
+    def digit(bit):
+        return (band // (1 << bit)) % 2
+
+    def across(bit):
+        return {"band": band + (1 - 2 * digit(bit)) * (1 << bit), "sub": sub}
+
+    barrier = pltpu.get_barrier_semaphore()
+    for peer in [core] + [across(bit) for bit in range(bits)]:
+        pl.semaphore_signal(barrier, inc=1, device_id=peer, device_id_type=pl.DeviceIdType.MESH)
+    pl.semaphore_wait(barrier, bits + 1)
+
+    started = []
+
+    def send(src, dst, send_at, recv_at, peer):
+        copy = pltpu.make_async_remote_copy(
+            src_ref=src, dst_ref=dst, send_sem=send_at, recv_sem=recv_at,
+            device_id=peer, device_id_type=pl.DeviceIdType.MESH,
+        )
+        copy.start()
+        started.append(copy)
+        return copy
+
+    def rows_at(start, size):
+        return pl.ds(pl.multiple_of(start, 16), size)
+
+    small_now[0] = small_ref[...]
+
+    def send_small(step, peer):
+        return send(
+            small_now.at[step], small_in.at[step], small_send.at[step], small_recv.at[step], peer
+        )
+
+    def add_small(step, copy):
+        copy.wait_recv()
+        small_now[step + 1] = small_now[step] + small_in[step]
+
+    small_copy = send_small(0, core)
+    first = []
+    place = 0
+    for h, (base, size) in enumerate(ranges):
+        half = size // 2
+        first.append(
+            (
+                place,
+                send(
+                    pack_ref.at[rows_at(base + (1 - sub) * half, half)],
+                    core_in.at[pl.ds(place, half)],
+                    send_sem.at[h, 0], recv_sem.at[h, 0], core,
+                ),
+            )
+        )
+        place += half
+    add_small(0, small_copy)
+    offset = []
+    for h, (base, size) in enumerate(ranges):
+        half = size // 2
+        place, copy = first[h]
+        at = base + sub * half
+        copy.wait_recv()
+        acc[rows_at(at, half), :] = pack_ref[rows_at(at, half), :] + core_in[place : place + half, :]
+        offset.append(at)
+
+    length = [size // 2 for _, size in ranges]
+    slot = 0
+    for step in range(bits):
+        flying = []
+        small_copy = send_small(step + 1, across(step))
+        for h in range(len(ranges)):
+            bit = (step + h) % bits
+            half = length[h] // 2
+            mine = digit(bit)
+            other = offset[h] + (1 - mine) * half
+            out_buf[slot : slot + half, :] = acc[rows_at(other, half), :].astype(BF16)
+            flying.append(
+                (
+                    slot,
+                    send(
+                        out_buf.at[pl.ds(slot, half)], in_buf.at[pl.ds(slot, half)],
+                        send_sem.at[h, step + 1], recv_sem.at[h, step + 1], across(bit),
+                    ),
+                )
+            )
+            offset[h] = offset[h] + mine * half
+            length[h] = half
+            slot += half
+        add_small(step + 1, small_copy)
+        for h in range(len(ranges)):
+            place, copy = flying[h]
+            copy.wait_recv()
+            rows = rows_at(offset[h], length[h])
+            value = acc[rows, :] + in_buf[place : place + length[h], :].astype(F32)
+            if step < bits - 1:
+                acc[rows, :] = value
+            else:
+                res[rows, :] = value.astype(BF16)
+
+    for step in range(bits + 1):
+        flying = []
+        for h in range(len(ranges)):
+            last = step == bits
+            bit = (bits - 1 - step + h) % bits
+            mine = sub if last else digit(bit)
+            rows = rows_at(offset[h], length[h])
+            at = bits + 1 + step
+            flying.append(
+                send(
+                    res.at[rows], res.at[rows], send_sem.at[h, at], recv_sem.at[h, at],
+                    core if last else across(bit),
+                )
+            )
+            offset[h] = offset[h] - mine * length[h]
+            length[h] = 2 * length[h]
+        for copy in flying:
+            copy.wait_recv()
+
+    small_out[...] = small_now[bits + 1]
+    width = pack_ref.shape[1]
+    hid = down_ref.shape[0]
+    chan = enc_ref.shape[0]
+    for k in range(hid // width):
+        up_ref[:, k * width : (k + 1) * width] = res[k * width : (k + 1) * width, :]
+    down_ref[...] = res[hid : 2 * hid, :]
+    at = 2 * hid
+    enc_ref[...] = res[at : at + 80, :][:chan]
+    dec_ref[...] = res[at + 80 : at + 160, :][:chan]
+    dw_ref[...] = res[at + 160 : at + 224, :][: dw_ref.shape[0]]
+    for copy in started:
+        copy.wait_send()
+
+
+def summed(pack, small, chan, hid):
+    total, width = pack.shape
+    band_size = lax.axis_size("band")
+    bits = band_size.bit_length() - 1
+    unit = 32 * band_size
+    front = -(-(total // unit) // 2) * unit
+    ranges = [(0, front)] if total == front else [(0, front), (front, total - front)]
+    parts = len(ranges)
+    staged = sum(size // 2 // (1 << (s + 1)) for _, size in ranges for s in range(bits))
+    vmem = pl.BlockSpec(memory_space=pltpu.VMEM)
+    dma = pltpu.SemaphoreType.DMA
+    up, down, enc, dw, dec, small = pl.pallas_call(
+        functools.partial(sum_kernel, ranges, band_size),
+        out_shape=(
+            jax.ShapeDtypeStruct((width, hid), BF16),
+            jax.ShapeDtypeStruct((hid, width), BF16),
+            jax.ShapeDtypeStruct((chan, width), BF16),
+            jax.ShapeDtypeStruct((KSIZE * KSIZE, width), BF16),
+            jax.ShapeDtypeStruct((chan, width), BF16),
+            jax.ShapeDtypeStruct((8, width), F32),
+        ),
+        in_specs=[vmem] * 2,
+        out_specs=(vmem,) * 6,
+        scratch_shapes=[
+            pltpu.VMEM((total, width), F32),
+            pltpu.VMEM((total // 2, width), F32),
+            pltpu.VMEM((staged, width), BF16),
+            pltpu.VMEM((staged, width), BF16),
+            pltpu.VMEM((total, width), BF16),
+            pltpu.VMEM((bits + 2, 8, width), F32),
+            pltpu.VMEM((bits + 1, 8, width), F32),
+            dma((parts, 2 * bits + 2)),
+            dma((parts, 2 * bits + 2)),
+            dma((bits + 1,)),
+            dma((bits + 1,)),
+        ],
+        compiler_params=pltpu.CompilerParams(
+            collective_id=0, has_side_effects=True, vmem_limit_bytes=40 * 1024 * 1024
+        ),
+        name="grad_sum",
+    )(pack, small)
+    return up, down, enc, dw, dec.T, small
+
+
 def shards(state, target, tile_plan, w_enc, dw_kernel, norm_gain, w_up, w_down, w_dec):
     chan, rows, cols = state.shape
     width, hid = w_up.shape
@@ -193,16 +376,18 @@
     wet = (plan >= 0).astype(F32)
     mask = jnp.pad(jnp.repeat(wet, PW, axis=1), ((0, 0), (0, LANES - cols)))
     inv_count = 1.0 / (jnp.sum((tile_plan >= 0).astype(F32)) * (chan * PW * PW))
-    pack_rows = 2 * hid + 80 + 80 + 56 + 8
+    members = lax.axis_size("band") * lax.axis_size("sub")
+    pack_rows = -(-(2 * hid + 80 + 80 + 64) // (16 * members)) * 16 * members
     vmem = pl.BlockSpec(memory_space=pltpu.VMEM)
-    pred, pack = pl.pallas_call(
+    pred, pack, small = pl.pallas_call(
         block_kernel,
         out_shape=(
             jax.ShapeDtypeStruct((rows, chan, LANES), BF16),
             jax.ShapeDtypeStruct((pack_rows, width), F32),
+            jax.ShapeDtypeStruct((8, width), F32),
         ),
         in_specs=[vmem] * 10,
-        out_specs=(vmem, vmem),
+        out_specs=(vmem,) * 3,
         scratch_shapes=[
             pltpu.VMEM((KSIZE, wide, LANES, width), F32),
             pltpu.VMEM((rows, LANES, width), F32),
@@ -219,18 +404,16 @@
         norm_gain.reshape(1, width), w_up, w_down, w_dec.T,
     )
     new_field = pred[:, :, :cols].transpose(1, 0, 2)
-    total = lax.psum(pack, ("band", "sub"))
-    g_up = jnp.concatenate([total[k * width : (k + 1) * width] for k in range(hid // width)], axis=1)
-    at = 2 * hid
+    g_up, g_down, g_enc, g_dw, g_dec, small = summed(pack, small, chan, hid)
     return (
         new_field,
-        (jnp.sum(total[at + 216]) * inv_count).reshape(1),
-        total[at : at + chan],
-        total[at + 160 : at + 160 + KSIZE * KSIZE],
-        total[at + 217],
-        g_up,
-        total[hid : 2 * hid],
-        total[at + 80 : at + 80 + chan].T,
+        (jnp.sum(small[0]) * inv_count).reshape(1),
+        g_enc.astype(F32),
+        g_dw.astype(F32),
+        small[1],
+        g_up.astype(F32),
+        g_down.astype(F32),
+        g_dec.astype(F32),
     )
 
 

time: 185 us -> 106 us (0.57)
  waiting for transfers between devices: 104 us -> 4.8 us
  Pallas kernels: 42.7 us -> 76.8 us
  between operations: 16.7 us -> 3.26 us
  other arithmetic: 7.33 us -> 9.41 us
  local copies, waits for them, and re-layouts: 6.82 us -> 4.85 us
    psum x1 -> x0, waiting for transfers between devices: 99.4 us -> none  [shards(): total = lax.psum(pack, ('band', 'sub'))]
    pallas_call x0 -> x1, Pallas kernels: none -> 34.4 us  [summed(): pl.pallas_call(functools.partial(sum_kernel, ranges, band_size), out_shap...]
    convert_element_type x0 -> x5, other arithmetic: none -> 4.04 us  [the longest x1 1.09 us: shards(): g_up.astype(F32)]
    slice x3 -> x0, local copies, waits for them, and re-layouts: 2.93 us -> none  [the longest x1 1.26 us: shards(): total[k * width:(k + 1) * width]]
  transfers between devices with their start and end apart: 5 -> 4, of which waited for: 3 -> 2; matrix products, arithmetic and copies ran while one was open for 3% -> 4% of each run, Pallas kernels for 0% -> 0%
where the time goes in v1:
time: 106 us
  Pallas kernels  76.8 us (72%)
  other arithmetic  9.41 us (9%)
  starting transfers between devices  6.74 us (6%)
  local copies, waits for them, and re-layouts  4.85 us (5%)
  waiting for transfers between devices  4.8 us (5%)
  between operations  3.26 us (3%)
    pallas_call x1, Pallas kernels, shards(): pl.pallas_call(block_kernel, out_shape=(jax.ShapeDtypeStruct((rows, chan,...  42.4 us
    pallas_call x1, Pallas kernels, summed(): pl.pallas_call(functools.partial(sum_kernel, ranges, band_size), out_shap...  34.4 us
    ppermute x4, starting transfers between devices, with_halo(): return (lax.ppermute(last, axis, up), lax.ppermute(leading, axis, down))  6.74 us
    ppermute x4, waiting for transfers between devices, with_halo(): return (lax.ppermute(last, axis, up), lax.ppermute(leading, axis, down))  4.8 us
  transfers between devices with their start and end apart: 4, of which 2 were waited for; matrix products, arithmetic and copies ran while one was open for 4% of the time, Pallas kernels for 0%

profile of v1, /device:TPU:0, one launch (start us, length us, event | category | flops | bytes accessed | tf_op | source)
XLA Modules:
  0.0 105.9 jit_solution(5902793857632233757)
XLA Ops:
  0.6 0.0 copy-start.5
  0.7 1.3 %fusion.1 = (bf16[77,12,3]{2,0,1:T(8,128)(2,1)S(1)}, bf16[77,12,3]{2,0,1:T(8,128)(2,1)S(1)}) fusion(bf16[77,12,120]{2,0,1:T(8,128)(2,1)} %param.9), kind=kLoop, calls=%fused_computation.12 | loop fusion | bytes 22176 | tf_op jit(solution)/shard_map/slice | solution.py:25
  2.0 0.5 collective-permute-start
  2.5 0.1 collective-permute-start.1
  2.6 1.3 %convert_reduce_fusion = f32[]{:T(128)} fusion(s32[8,20]{1,0:T(8,128)} %param.11), kind=kLoop, calls=%fused_computation.7 | loop fusion | flops 479 | bytes 644 | tf_op jit(solution)/shard_map/reduce_sum | solution.py:378
  3.8 0.8 fusion
  4.6 0.1 broadcast_in_dim.9
  4.7 0.1 broadcast_in_dim.10
  4.8 0.8 convert_element_type.36.dw_ref
  6.2 1.0 pad.8.goal_ref
  7.2 0.0 collective-permute-done
  7.2 0.0 collective-permute-done.1
  7.3 1.0 pad_maximum_fusion.3
  8.3 4.9 %collective-permute-start.2 = (bf16[77,3,128]{2,0,1:T(8,128)(2,1)S(1)}, bf16[77,3,128]{2,0,1:T(8,128)(2,1)S(1)}, u32[]{:S(2)}, u32[]{:S(2)}) collective-permute-start(bf16[77,3,128]{2,0,1:T(8,128)(2,1)S(1)} %get-tuple-element.26), channel_id=1, source_target_pairs={{0,2},{2,4},{4,6},{6,8},{8,10},{10,12},{12,14},{1,3},{3,5},{5,7},{... | collective-permute-start | bytes 177416 | tf_op jit(solution)/shard_map/ppermute | solution.py:27
  13.2 1.3 %collective-permute-start.3 = (bf16[77,3,128]{2,0,1:T(8,128)(2,1)S(1)}, bf16[77,3,128]{2,0,1:T(8,128)(2,1)S(1)}, u32[]{:S(2)}, u32[]{:S(2)}) collective-permute-start(bf16[77,3,128]{2,0,1:T(8,128)(2,1)S(1)} %get-tuple-element.27), channel_id=1, source_target_pairs={{2,0},{4,2},{6,4},{8,6},{10,8},{12,10},{14,12},{3,1},{5,3},{7,5},{... | collective-permute-start | bytes 177416 | tf_op jit(solution)/shard_map/ppermute | solution.py:27
  14.5 0.5 collective-permute-done.2
  15.0 4.3 %collective-permute-done.3 = bf16[77,3,128]{2,0,1:T(8,128)(2,1)S(1)} collective-permute-done((bf16[77,3,128]{2,0,1:T(8,128)(2,1)S(1)}, bf16[77,3,128]{2,0,1:T(8,128)(2,1)S(1)}, u32[]{:S(2)}, u32[]{:S(2)}) %collective-permute-start.3) | collective-permute-done | bytes 59168 | tf_op jit(solution)/shard_map/ppermute | solution.py:27
  19.3 0.3 maximum_bitcast_fusion.x_ref
  19.7 0.0 copy-done.3
  19.7 0.0 copy-done.1
  19.7 0.0 copy-done.4
  19.7 0.0 copy-done.2
  19.7 42.4 %block.1 = (bf16[12,77,128]{2,1,0:T(8,128)(2,1)S(1)}, f32[2304,256]{1,0:T(8,128)}, f32[8,256]{1,0:T(8,128)S(1)}) custom-call(bf16[18,77,128]{2,1,0:T(8,128)(2,1)S(1)} %maximum_bitcast_fusion.x_ref, bf16[12,77,128]{2,1,0:T(8,128)(2,1)S(1)} %pad.8.goal_ref, f32[1,128]{1,0:T(1,128)S(1)} %get-tuple-element.33.mask_ref, ...), custom_call_target="tpu_custom_call" | custom-call | tf_op jit(solution)/shard_map/block/pallas_call | solution.py:382
  62.1 0.7 slice_bitcast_fusion
  62.8 1.7 %copy-done = f32[2304,256]{1,0:T(8,128)S(1)} copy-done((f32[2304,256]{1,0:T(8,128)S(1)}, f32[2304,256]{1,0:T(8,128)}, u32[]{:S(2)}) %copy-start) | copy-done | bytes 2359320
  64.5 34.4 %grad_sum.1 = (bf16[256,1024]{1,0:T(8,128)(2,1)S(1)}, bf16[1024,256]{1,0:T(8,128)(2,1)S(1)}, bf16[77,256]{1,0:T(8,128)(2,1)S(1)}, bf16[49,256]{1,0:T(8,128)(2,1)...) custom-call(f32[2304,256]{1,0:T(8,128)S(1)} %copy-done, f32[8,256]{1,0:T(8,128)S(1)} %get-tuple-element.19.small_ref), custom_call_target="tpu_custom_call" | custom-call | tf_op jit(solution)/shard_map/grad_sum/pallas_call | solution.py:329
  98.9 1.2 %fusion.2 = (f32[1,256]{1,0:T(1,128)}, f32[]{:T(128)}) fusion(f32[8,256]{1,0:T(8,128)S(1)} %get-tuple-element.20), kind=kLoop, calls=%fused_computation.13 | loop fusion | flops 255 | bytes 3076 | tf_op jit(solution)/shard_map/slice | solution.py:413
  100.7 0.6 convert_element_type.38
  101.3 0.6 convert_element_type.37
  102.0 0.6 convert_bitcast_fusion
  102.6 1.1 %convert_element_type.39 = f32[256,1024]{1,0:T(8,128)} convert(bf16[256,1024]{1,0:T(8,128)(2,1)S(1)} %get-tuple-element.23) | non-fusion elementwise | flops 262144 | bytes 1572864 | tf_op jit(solution)/shard_map/convert_element_type | solution.py:414
  103.7 1.0 convert_element_type.40
  (8 shorter events, 0.1 us)
Async XLA Ops:
  0.6 18.7 %copy-start.5 = (bf16[77,12,120]{2,0,1:T(8,128)(2,1)S(1)}, bf16[77,12,120]{2,0,1:T(8,128)(2,1)}, u32[]{:S(2)}) copy-start(bf16[77,12,120]{2,0,1:T(8,128)(2,1)} %param.9) | copy-start | bytes 665284
  0.6 19.0 %copy-start.3 = (bf16[256,77]{0,1:T(8,128)(2,1)S(1)}, bf16[256,77]{0,1:T(8,128)(2,1)}, u32[]{:S(2)}) copy-start(bf16[256,77]{0,1:T(8,128)(2,1)} %param.17) | copy-start | bytes 118276
  0.7 19.0 %copy-start.1 = (bf16[256,1024]{1,0:T(8,128)(2,1)S(1)}, bf16[256,1024]{1,0:T(8,128)(2,1)}, u32[]{:S(2)}) copy-start(bf16[256,1024]{1,0:T(8,128)(2,1)} %w_up_ref.1) | copy-start | bytes 1572868
  0.7 19.0 %copy-start.4 = (f32[256]{0:T(256)S(1)}, f32[256]{0:T(256)}, u32[]{:S(2)}) copy-start(f32[256]{0:T(256)} %param.14) | copy-start | bytes 3076
  0.7 19.0 %copy-start.2 = (bf16[77,256]{1,0:T(8,128)(2,1)S(1)}, bf16[77,256]{1,0:T(8,128)(2,1)}, u32[]{:S(2)}) copy-start(bf16[77,256]{1,0:T(8,128)(2,1)} %w_enc_ref.1) | copy-start | bytes 118276
  2.0 5.3 %collective-permute-start = (bf16[77,12,3]{2,0,1:T(8,128)(2,1)S(1)}, bf16[77,12,3]{2,0,1:T(8,128)(2,1)S(1)}, u32[]{:S(2)}, u32[]{:S(2)}) collective-permute-start(bf16[77,12,3]{2,0,1:T(8,128)(2,1)S(1)} %get-tuple-element.28), channel_id=1, source_target_pairs={{0,1},{1,0},{2,3},{3,2},{4,5},{5,4},{6,7},{7,6},{8,9},{9,8},{10,11... | collective-permute-start | bytes 16640 | tf_op jit(solution)/shard_map/ppermute | solution.py:27
  2.5 4.8 %collective-permute-start.1 = (bf16[77,12,3]{2,0,1:T(8,128)(2,1)S(1)}, bf16[77,12,3]{2,0,1:T(8,128)(2,1)S(1)}, u32[]{:S(2)}, u32[]{:S(2)}) collective-permute-start(bf16[77,12,3]{2,0,1:T(8,128)(2,1)S(1)} %get-tuple-element.29), channel_id=1, source_target_pairs={{1,0},{0,1},{3,2},{2,3},{5,4},{4,5},{7,6},{6,7},{9,8},{8,9},{11,10... | collective-permute-start | bytes 16640 | tf_op jit(solution)/shard_map/ppermute | solution.py:27
  8.3 6.7 %collective-permute-start.2 = (bf16[77,3,128]{2,0,1:T(8,128)(2,1)S(1)}, bf16[77,3,128]{2,0,1:T(8,128)(2,1)S(1)}, u32[]{:S(2)}, u32[]{:S(2)}) collective-permute-start(bf16[77,3,128]{2,0,1:T(8,128)(2,1)S(1)} %get-tuple-element.26), channel_id=1, source_target_pairs={{0,2},{2,4},{4,6},{6,8},{8,10},{10,12},{12,14},{1,3},{3,5},{5,7},{... | collective-permute-start | bytes 177416 | tf_op jit(solution)/shard_map/ppermute | solution.py:27
  13.2 6.1 %collective-permute-start.3 = (bf16[77,3,128]{2,0,1:T(8,128)(2,1)S(1)}, bf16[77,3,128]{2,0,1:T(8,128)(2,1)S(1)}, u32[]{:S(2)}, u32[]{:S(2)}) collective-permute-start(bf16[77,3,128]{2,0,1:T(8,128)(2,1)S(1)} %get-tuple-element.27), channel_id=1, source_target_pairs={{2,0},{4,2},{6,4},{8,6},{10,8},{12,10},{14,12},{3,1},{5,3},{7,5},{... | collective-permute-start | bytes 177416 | tf_op jit(solution)/shard_map/ppermute | solution.py:27
  62.8 1.7 %copy-start = (f32[2304,256]{1,0:T(8,128)S(1)}, f32[2304,256]{1,0:T(8,128)}, u32[]{:S(2)}) copy-start(f32[2304,256]{1,0:T(8,128)} %get-tuple-element.18.pack_ref) | copy-start | bytes 7077892

commit v2 on v0

--- a/solution.py
+++ b/solution.py
@@ -31,9 +31,15 @@
     return lax.dot_general(left, right, ((dims[:1], dims[1:]), ((), ())), preferred_element_type=F32)
 
 
+def rows_at(start, size):
+    return pl.ds(pl.multiple_of(start, 16), size)
+
+
 def block_kernel(
-    x_ref, goal_ref, mask_ref, gscale_ref, w_enc_ref, dw_ref, gain_ref, w_up_ref, w_down_ref,
-    w_dec_t_ref, pred_ref, pack_ref, shifted, conv, gres_all, taps, dk, up_acc, down_acc,
+    ranges, band_size, x_ref, goal_ref, mask_ref, gscale_ref, w_enc_ref, dw_ref, gain_ref, w_up_ref,
+    w_down_ref, w_dec_t_ref, pred_ref, small_out, up_ref, down_ref, enc_ref, dw_out, dec_ref,
+    shifted, conv, gres_all, taps, dk, up_acc, down_acc, acc, core_in, out_buf, in_buf, res,
+    small_now, small_in, send_sem, recv_sem, small_send, small_recv,
 ):
     chan = x_ref.shape[1]
     width = w_enc_ref.shape[1]
@@ -42,11 +48,123 @@
     wide = rows + KSIZE - 1
     groups = (LANES - 8) // 8
     lane_parts = width // LANES
-    base_down = hid
     base_enc = 2 * hid
     base_dec = base_enc + 80
     base_dw = base_dec + 80
-    base_small = base_dw + 56
+
+    band = lax.axis_index("band")
+    sub = lax.axis_index("sub")
+    bits = band_size.bit_length() - 1
+    core = {"band": band, "sub": 1 - sub}
+    started = []
+
+    def digit(bit):
+        return (band // (1 << bit)) % 2
+
+    def across(bit):
+        return {"band": band + (1 - 2 * digit(bit)) * (1 << bit), "sub": sub}
+
+    barrier = pltpu.get_barrier_semaphore()
+    for peer in [core] + [across(bit) for bit in range(bits)]:
+        pl.semaphore_signal(barrier, inc=1, device_id=peer, device_id_type=pl.DeviceIdType.MESH)
+
+    def send(src, dst, send_at, recv_at, peer):
+        copy = pltpu.make_async_remote_copy(
+            src_ref=src, dst_ref=dst, send_sem=send_at, recv_sem=recv_at,
+            device_id=peer, device_id_type=pl.DeviceIdType.MESH,
+        )
+        copy.start()
+        started.append(copy)
+        return copy
+
+    def send_small(step, peer):
+        return send(
+            small_now.at[step], small_in.at[step], small_send.at[step], small_recv.at[step], peer
+        )
+
+    def add_small(step, copy):
+        copy.wait_recv()
+        small_now[step + 1] = small_now[step] + small_in[step]
+
+    def exchange(parts, with_small):
+        small_copy = send_small(0, core) if with_small else None
+        first = []
+        offset = {}
+        length = {}
+        for h in parts:
+            base, size, core_at, _ = ranges[h]
+            half = size // 2
+            first.append(
+                send(
+                    acc.at[rows_at(base + (1 - sub) * half, half)],
+                    core_in.at[pl.ds(core_at, half)],
+                    send_sem.at[h, 0], recv_sem.at[h, 0], core,
+                )
+            )
+            offset[h] = base + sub * half
+            length[h] = half
+        yield
+        if with_small:
+            add_small(0, small_copy)
+        for h, copy in zip(parts, first):
+            copy.wait_recv()
+            at = rows_at(offset[h], length[h])
+            core_at = ranges[h][2]
+            acc[at, :] = acc[at, :] + core_in[core_at : core_at + length[h], :]
+        slots = {h: ranges[h][3] for h in parts}
+        for step in range(bits):
+            flying = []
+            if with_small:
+                small_copy = send_small(step + 1, across(step))
+            for h in parts:
+                bit = (step + h) % bits
+                half = length[h] // 2
+                mine = digit(bit)
+                slot = slots[h]
+                other = offset[h] + (1 - mine) * half
+                out_buf[slot : slot + half, :] = acc[rows_at(other, half), :].astype(BF16)
+                flying.append(
+                    (
+                        slot,
+                        send(
+                            out_buf.at[pl.ds(slot, half)], in_buf.at[pl.ds(slot, half)],
+                            send_sem.at[h, step + 1], recv_sem.at[h, step + 1], across(bit),
+                        ),
+                    )
+                )
+                offset[h] = offset[h] + mine * half
+                length[h] = half
+                slots[h] = slot + half
+            yield
+            if with_small:
+                add_small(step + 1, small_copy)
+            for h, (place, copy) in zip(parts, flying):
+                copy.wait_recv()
+                at = rows_at(offset[h], length[h])
+                value = acc[at, :] + in_buf[place : place + length[h], :].astype(F32)
+                if step < bits - 1:
+                    acc[at, :] = value
+                else:
+                    res[at, :] = value.astype(BF16)
+        for step in range(bits + 1):
+            flying = []
+            for h in parts:
+                last = step == bits
+                bit = (bits - 1 - step + h) % bits
+                mine = sub if last else digit(bit)
+                at = rows_at(offset[h], length[h])
+                sem = bits + 1 + step
+                flying.append(
+                    send(
+                        res.at[at], res.at[at], send_sem.at[h, sem], recv_sem.at[h, sem],
+                        core if last else across(bit),
+                    )
+                )
+                offset[h] = offset[h] - mine * length[h]
+                length[h] = 2 * length[h]
+            yield
+            for copy in flying:
+                copy.wait_recv()
 
     for i in range(KSIZE * KSIZE):
         taps[i] = jnp.broadcast_to(dw_ref[i : i + 1, :], (8, width))
@@ -54,7 +172,8 @@
     up_acc[...] = jnp.zeros_like(up_acc)
     down_acc[...] = jnp.zeros_like(down_acc)
     gres_all[...] = jnp.zeros_like(gres_all)
-    pack_ref[base_enc:, :] = jnp.zeros((pack_ref.shape[0] - base_enc, width), F32)
+    acc[base_enc:, :] = jnp.zeros((acc.shape[0] - base_enc, width), F32)
+    small_now[0] = jnp.zeros((8, width), F32)
     inside = lax.broadcasted_iota(jnp.int32, (LANES, width), 0) < groups * 8
 
     @pl.loop(0, wide)
@@ -66,22 +185,21 @@
 
     conv[:, groups * 8 :, :] = jnp.zeros((rows, LANES - groups * 8, width), F32)
 
-    @pl.loop(0, groups * lane_parts)
-    def _(step):
-        at = (
+    def part_of(step):
+        return (
             pl.ds(pl.multiple_of((step // lane_parts) * 8, 8), 8),
             pl.ds(pl.multiple_of((step % lane_parts) * LANES, LANES), LANES),
         )
-        acc = [None] * rows
+
+    @pl.loop(0, groups * lane_parts)
+    def _(step):
+        at = part_of(step)
+        total = jnp.zeros((rows, 8, LANES), F32)
         for b in range(KSIZE):
-            line = [shifted[(b, r) + at] for r in range(wide)]
+            line = shifted[(b, slice(None)) + at]
             for a in range(KSIZE):
-                tap = taps[a * KSIZE + b, :, at[1]]
-                for y in range(rows):
-                    term = line[y + a] * tap
-                    acc[y] = term if acc[y] is None else acc[y] + term
-        for y in range(rows):
-            conv[(y,) + at] = acc[y]
+                total = total + line[a : a + rows] * taps[a * KSIZE + b, :, at[1]][None]
+        conv[(slice(None),) + at] = total
 
     gain = gain_ref[...]
     mask = jnp.concatenate([mask_ref[...]] * 2, axis=1)
@@ -117,18 +235,16 @@
         pred_ref[y] = keep[:, :LANES]
         pred_ref[y + 1] = keep[:, LANES:]
         misfit = (pred - goal) * mask
-        pack_ref[base_small : base_small + 1, :] += jnp.sum(misfit * misfit, axis=0, keepdims=True)
+        small_now[0, 0:1, :] += jnp.sum(misfit * misfit, axis=0, keepdims=True)
         gout = (misfit * gscale).astype(BF16)
-        pack_ref[base_dec : base_dec + chan, :] += dot(gout, residual, (1, 0))
+        acc[base_dec : base_dec + chan, :] += dot(gout, residual, (1, 0))
         gres = dot(gout, w_dec_t_ref[...], (0, 0)).astype(BF16)
         gres_all[pl.ds(y + RIM, 2)] = gres.astype(F32).reshape(2, LANES, width)
         down_acc[...] += dot(gres, act, (0, 0))
         gpre = (dot(gres, w_down_ref[...], (1, 1)) * slope).astype(BF16)
         up_acc[...] += dot(scaled, gpre, (0, 0))
         gscaled = dot(gpre, w_up_ref[...], (1, 1))
-        pack_ref[base_small + 1 : base_small + 2, :] += jnp.sum(
-            gscaled * normed, axis=0, keepdims=True
-        )
+        small_now[0, 1:2, :] += jnp.sum(gscaled * normed, axis=0, keepdims=True)
         g = gscaled * gain
         gconv = inv_std * (
             g
@@ -137,43 +253,64 @@
         )
         conv[pl.ds(y, 2)] = gconv.reshape(2, LANES, width)
 
-    @pl.loop(0, groups * lane_parts)
-    def _(step):
-        at = (
-            pl.ds(pl.multiple_of((step // lane_parts) * 8, 8), 8),
-            pl.ds(pl.multiple_of((step % lane_parts) * LANES, LANES), LANES),
-        )
-        gc = [conv[(y,) + at] for y in range(rows)]
+    for k in range(hid // width):
+        cols = slice(k * width, (k + 1) * width)
+        acc[cols, :] = up_acc[:, cols]
+        acc[hid + k * width : hid + (k + 1) * width, :] = down_acc[:, cols].T
+
+    pl.semaphore_wait(barrier, bits + 1)
+    flow = exchange([0, 1], True)
+    next(flow)
+
+    def depthwise_back(step):
+        at = part_of(step)
+        gc = conv[(slice(None),) + at]
+        gc_rows = [gc[y] for y in range(rows)]
         for b in range(KSIZE):
-            line = [shifted[(b, r) + at] for r in range(wide)]
+            line = shifted[(b, slice(None)) + at]
             for a in range(KSIZE):
-                total = gc[0] * line[a]
-                for y in range(1, rows):
-                    total = total + gc[y] * line[y + a]
-                dk[a * KSIZE + b, :, at[1]] += total
+                dk[a * KSIZE + b, :, at[1]] += jnp.sum(gc * line[a : a + rows], axis=0)
             spread = [None] * wide
             for a in range(KSIZE):
                 tap = taps[a * KSIZE + b, :, at[1]]
                 for y in range(rows):
-                    term = gc[y] * tap
+                    term = gc_rows[y] * tap
                     old = spread[y + a]
                     spread[y + a] = term if old is None else old + term
             for r in range(wide):
                 shifted[(b, r) + at] = spread[r]
 
-    @pl.loop(0, wide)
-    def _(r):
+    def encoder_back(r):
         g = pltpu.roll(gres_all[r], RIM, 0) + shifted[0, r]
         for b in range(1, KSIZE):
             g = g + pltpu.roll(shifted[b, r], b, 0)
-        pack_ref[base_enc : base_enc + chan, :] += dot(x_ref[r], g.astype(BF16), (1, 0))
-
+        acc[base_enc : base_enc + chan, :] += dot(x_ref[r], g.astype(BF16), (1, 0))
+
+    steps = groups * lane_parts
+    for piece in range(6):
+        pl.loop(piece * steps // 6, (piece + 1) * steps // 6)(depthwise_back)
+        next(flow, None)
+    for piece in range(2):
+        pl.loop(piece * wide // 2, (piece + 1) * wide // 2)(encoder_back)
+        next(flow, None)
     for i in range(KSIZE * KSIZE):
-        pack_ref[base_dw + i : base_dw + i + 1, :] = jnp.sum(dk[i], axis=0, keepdims=True)
+        acc[base_dw + i : base_dw + i + 1, :] = jnp.sum(dk[i], axis=0, keepdims=True)
+    for _ in flow:
+        pass
+
+    tail = exchange([2], False)
+    next(tail)
+    small_out[...] = small_now[bits + 1]
     for k in range(hid // width):
-        cols = slice(k * width, (k + 1) * width)
-        pack_ref[cols, :] = up_acc[:, cols]
-        pack_ref[base_down + k * width : base_down + (k + 1) * width, :] = down_acc[:, cols].T
+        up_ref[:, k * width : (k + 1) * width] = res[k * width : (k + 1) * width, :]
+    down_ref[...] = res[hid : 2 * hid, :]
+    for _ in tail:
+        pass
+    enc_ref[...] = res[base_enc : base_enc + 80, :][:chan]
+    dec_ref[...] = res[base_dec : base_dec + 80, :][:chan]
+    dw_out[...] = res[base_dw : base_dw + 64, :][: dw_out.shape[0]]
+    for copy in started:
+        copy.wait_send()
 
 
 def shards(state, target, tile_plan, w_enc, dw_kernel, norm_gain, w_up, w_down, w_dec):
@@ -193,16 +330,31 @@
     wet = (plan >= 0).astype(F32)
     mask = jnp.pad(jnp.repeat(wet, PW, axis=1), ((0, 0), (0, LANES - cols)))
     inv_count = 1.0 / (jnp.sum((tile_plan >= 0).astype(F32)) * (chan * PW * PW))
-    pack_rows = 2 * hid + 80 + 80 + 56 + 8
+    band_size = lax.axis_size("band")
+    bits = band_size.bit_length() - 1
+    unit = 32 * band_size
+    cuts = [hid, hid, -(-(80 + 80 + 64) // unit) * unit]
+    ranges = []
+    base = staged = 0
+    for size in cuts:
+        ranges.append((base, size, base // 2, staged))
+        base += size
+        staged += sum(size // 2 // (1 << (s + 1)) for s in range(bits))
     vmem = pl.BlockSpec(memory_space=pltpu.VMEM)
-    pred, pack = pl.pallas_call(
-        block_kernel,
+    dma = pltpu.SemaphoreType.DMA
+    pred, small, g_up, g_down, g_enc, g_dw, g_dec = pl.pallas_call(
+        functools.partial(block_kernel, ranges, band_size),
         out_shape=(
             jax.ShapeDtypeStruct((rows, chan, LANES), BF16),
-            jax.ShapeDtypeStruct((pack_rows, width), F32),
+            jax.ShapeDtypeStruct((8, width), F32),
+            jax.ShapeDtypeStruct((width, hid), BF16),
+            jax.ShapeDtypeStruct((hid, width), BF16),
+            jax.ShapeDtypeStruct((chan, width), BF16),
+            jax.ShapeDtypeStruct((KSIZE * KSIZE, width), BF16),
+            jax.ShapeDtypeStruct((chan, width), BF16),
         ),
         in_specs=[vmem] * 10,
-        out_specs=(vmem, vmem),
+        out_specs=(vmem,) * 7,
         scratch_shapes=[
             pltpu.VMEM((KSIZE, wide, LANES, width), F32),
             pltpu.VMEM((rows, LANES, width), F32),
@@ -211,26 +363,36 @@
             pltpu.VMEM((KSIZE * KSIZE, 8, width), F32),
             pltpu.VMEM((width, hid), F32),
             pltpu.VMEM((width, hid), F32),
+            pltpu.VMEM((base, width), F32),
+            pltpu.VMEM((base // 2, width), F32),
+            pltpu.VMEM((staged, width), BF16),
+            pltpu.VMEM((staged, width), BF16),
+            pltpu.VMEM((base, width), BF16),
+            pltpu.VMEM((bits + 2, 8, width), F32),
+            pltpu.VMEM((bits + 1, 8, width), F32),
+            dma((3, 2 * bits + 2)),
+            dma((3, 2 * bits + 2)),
+            dma((bits + 1,)),
+            dma((bits + 1,)),
         ],
-        compiler_params=pltpu.CompilerParams(vmem_limit_bytes=52 * 1024 * 1024),
+        compiler_params=pltpu.CompilerParams(
+            collective_id=0, has_side_effects=True, vmem_limit_bytes=52 * 1024 * 1024
+        ),
         name="block",
     )(
         x, goal, mask, mask * (2.0 * inv_count), w_enc, dw_kernel.astype(F32),
         norm_gain.reshape(1, width), w_up, w_down, w_dec.T,
     )
     new_field = pred[:, :, :cols].transpose(1, 0, 2)
-    total = lax.psum(pack, ("band", "sub"))
-    g_up = jnp.concatenate([total[k * width : (k + 1) * width] for k in range(hid // width)], axis=1)
-    at = 2 * hid
     return (
         new_field,
-        (jnp.sum(total[at + 216]) * inv_count).reshape(1),
-        total[at : at + chan],
-        total[at + 160 : at + 160 + KSIZE * KSIZE],
-        total[at + 217],
-        g_up,
-        total[hid : 2 * hid],
-        total[at + 80 : at + 80 + chan].T,
+        (jnp.sum(small[0]) * inv_count).reshape(1),
+        g_enc.astype(F32),
+        g_dw.astype(F32),
+        small[1],
+        g_up.astype(F32),
+        g_down.astype(F32),
+        g_dec.T.astype(F32),
     )
 
 

time: 185 us -> 107 us (0.58)
  waiting for transfers between devices: 104 us -> 4.78 us
  Pallas kernels: 42.7 us -> 81.6 us
  between operations: 16.7 us -> 3.28 us
  local copies, waits for them, and re-layouts: 6.82 us -> 3.75 us
    psum x1 -> x0, waiting for transfers between devices: 99.4 us -> none  [shards(): total = lax.psum(pack, ('band', 'sub'))]
    pallas_call x1, Pallas kernels: 42.7 us -> 81.6 us  [shards(): pl.pallas_call(functools.partial(block_kernel, ranges, band_size), out_sh...]
    convert_element_type x0 -> x5, other arithmetic: none -> 4.04 us  [the longest x1 1.09 us: shards(): g_up.astype(F32)]
    slice x3 -> x0, local copies, waits for them, and re-layouts: 2.93 us -> none  [the longest x1 1.26 us: shards(): total[k * width:(k + 1) * width]]
  transfers between devices with their start and end apart: 5 -> 4, of which waited for: 3 -> 2; matrix products, arithmetic and copies ran while one was open for 3% -> 1% of each run, Pallas kernels for 0% -> 0%
where the time goes in v2:
time: 107 us
  Pallas kernels  81.6 us (76%)
  starting transfers between devices  6.74 us (6%)
  other arithmetic  6.42 us (6%)
  waiting for transfers between devices  4.78 us (4%)
  local copies, waits for them, and re-layouts  3.75 us (4%)
  between operations  3.28 us (3%)
    pallas_call x1, Pallas kernels, shards(): pl.pallas_call(functools.partial(block_kernel, ranges, band_size), out_sh...  81.6 us
    ppermute x4, starting transfers between devices, with_halo(): return (lax.ppermute(last, axis, up), lax.ppermute(leading, axis, down))  6.74 us
    ppermute x4, waiting for transfers between devices, with_halo(): return (lax.ppermute(last, axis, up), lax.ppermute(leading, axis, down))  4.78 us
  transfers between devices with their start and end apart: 4, of which 2 were waited for; matrix products, arithmetic and copies ran while one was open for 1% of the time, Pallas kernels for 0%

profile of v2, /device:TPU:0, one launch (start us, length us, event | category | flops | bytes accessed | tf_op | source)
XLA Modules:
  0.0 106.6 jit_solution(3357150174682007738)
XLA Ops:
  0.7 1.2 %fusion.1 = (bf16[77,12,3]{2,0,1:T(8,128)(2,1)S(1)}, bf16[77,12,3]{2,0,1:T(8,128)(2,1)S(1)}) fusion(bf16[77,12,120]{2,0,1:T(8,128)(2,1)} %param.9), kind=kLoop, calls=%fused_computation.12 | loop fusion | bytes 22176 | tf_op jit(solution)/shard_map/slice | solution.py:25
  1.9 0.0 copy-start.6
  1.9 0.5 collective-permute-start
  2.4 0.1 collective-permute-start.1
  2.5 0.6 convert_reduce_fusion
  3.1 0.1 fusion
  3.2 0.1 broadcast_in_dim.9
  3.3 0.1 broadcast_in_dim.10
  4.0 0.0 copy-done.5
  4.1 0.1 pad.8.goal_ref
  4.1 0.0 copy-start.3
  4.1 0.0 collective-permute-done
  4.1 0.0 collective-permute-done.1
  4.2 0.9 copy-done.3
  5.1 0.2 pad_maximum_fusion.3
  5.3 4.9 %collective-permute-start.2 = (bf16[77,3,128]{2,0,1:T(8,128)(2,1)S(1)}, bf16[77,3,128]{2,0,1:T(8,128)(2,1)S(1)}, u32[]{:S(2)}, u32[]{:S(2)}) collective-permute-start(bf16[77,3,128]{2,0,1:T(8,128)(2,1)S(1)} %get-tuple-element.22), channel_id=1, source_target_pairs={{0,2},{2,4},{4,6},{6,8},{8,10},{10,12},{12,14},{1,3},{3,5},{5,7},{... | collective-permute-start | bytes 177416 | tf_op jit(solution)/shard_map/ppermute | solution.py:27
  10.1 1.3 %collective-permute-start.3 = (bf16[77,3,128]{2,0,1:T(8,128)(2,1)S(1)}, bf16[77,3,128]{2,0,1:T(8,128)(2,1)S(1)}, u32[]{:S(2)}, u32[]{:S(2)}) collective-permute-start(bf16[77,3,128]{2,0,1:T(8,128)(2,1)S(1)} %get-tuple-element.23), channel_id=1, source_target_pairs={{2,0},{4,2},{6,4},{8,6},{10,8},{12,10},{14,12},{3,1},{5,3},{7,5},{... | collective-permute-start | bytes 177416 | tf_op jit(solution)/shard_map/ppermute | solution.py:27
  11.4 0.0 copy-start
  11.4 0.0 copy-start.1
  11.5 0.5 collective-permute-done.2
  12.0 4.3 %collective-permute-done.3 = bf16[77,3,128]{2,0,1:T(8,128)(2,1)S(1)} collective-permute-done((bf16[77,3,128]{2,0,1:T(8,128)(2,1)S(1)}, bf16[77,3,128]{2,0,1:T(8,128)(2,1)S(1)}, u32[]{:S(2)}, u32[]{:S(2)}) %collective-permute-start.3) | collective-permute-done | bytes 59168 | tf_op jit(solution)/shard_map/ppermute | solution.py:27
  16.2 0.3 maximum_bitcast_fusion.x_ref
  16.6 0.0 copy-start.2
  16.6 0.7 copy-done.2
  17.3 81.6 %block.1 = (bf16[12,77,128]{2,1,0:T(8,128)(2,1)S(1)}, f32[8,256]{1,0:T(8,128)S(1)}, bf16[256,1024]{1,0:T(8,128)(2,1)S(1)}, bf16[1024,256]{1,0:T(8,128)(2,1)}, bf...) custom-call(bf16[18,77,128]{2,1,0:T(8,128)(2,1)S(1)} %maximum_bitcast_fusion.x_ref, ...), custom_call_target="tpu_custom_call" | custom-call | tf_op jit(solution)/shard_map/block/pallas_call | solution.py:345
  98.9 1.2 %fusion.2 = (f32[1,256]{1,0:T(1,128)}, f32[]{:T(128)}) fusion(f32[8,256]{1,0:T(8,128)S(1)} %get-tuple-element.16), kind=kLoop, calls=%fused_computation.13 | loop fusion | flops 255 | bytes 3076 | tf_op jit(solution)/shard_map/slice | solution.py:392
  100.7 1.1 %convert_element_type.39 = f32[256,1024]{1,0:T(8,128)} convert(bf16[256,1024]{1,0:T(8,128)(2,1)S(1)} %get-tuple-element.19) | non-fusion elementwise | flops 262144 | bytes 1572864 | tf_op jit(solution)/shard_map/convert_element_type | solution.py:393
  101.8 1.0 convert_element_type.40
  102.8 0.7 slice_bitcast_fusion
  103.6 0.6 convert_bitcast_fusion
  104.2 0.6 convert_element_type.37
  104.8 0.6 convert_element_type.38
  (11 shorter events, 0.1 us)
Async XLA Ops:
  0.6 1.9 %copy-start.7 = (s32[8,20]{1,0:T(8,128)S(1)}, s32[8,20]{1,0:T(8,128)}, u32[]{:S(2)}) copy-start(s32[8,20]{1,0:T(8,128)} %param.11) | copy-start | bytes 1924
  0.6 3.4 %copy-start.5 = (bf16[77,12,120]{2,0,1:T(8,128)(2,1)S(1)}, bf16[77,12,120]{2,0,1:T(8,128)(2,1)}, u32[]{:S(2)}) copy-start(bf16[77,12,120]{2,0,1:T(8,128)(2,1)} %param.10) | copy-start | bytes 665284
  1.9 1.4 %copy-start.6 = (bf16[49,256]{1,0:T(8,128)(2,1)S(1)}, bf16[49,256]{1,0:T(8,128)(2,1)}, u32[]{:S(2)}) copy-start(bf16[49,256]{1,0:T(8,128)(2,1)} %param.13) | copy-start | bytes 75268
  1.9 2.2 %collective-permute-start = (bf16[77,12,3]{2,0,1:T(8,128)(2,1)S(1)}, bf16[77,12,3]{2,0,1:T(8,128)(2,1)S(1)}, u32[]{:S(2)}, u32[]{:S(2)}) collective-permute-start(bf16[77,12,3]{2,0,1:T(8,128)(2,1)S(1)} %get-tuple-element.24), channel_id=1, source_target_pairs={{0,1},{1,0},{2,3},{3,2},{4,5},{5,4},{6,7},{7,6},{8,9},{9,8},{10,11... | collective-permute-start | bytes 16640 | tf_op jit(solution)/shard_map/ppermute | solution.py:27
  2.4 1.7 %collective-permute-start.1 = (bf16[77,12,3]{2,0,1:T(8,128)(2,1)S(1)}, bf16[77,12,3]{2,0,1:T(8,128)(2,1)S(1)}, u32[]{:S(2)}, u32[]{:S(2)}) collective-permute-start(bf16[77,12,3]{2,0,1:T(8,128)(2,1)S(1)} %get-tuple-element.25), channel_id=1, source_target_pairs={{1,0},{0,1},{3,2},{2,3},{5,4},{4,5},{7,6},{6,7},{9,8},{8,9},{11,10... | collective-permute-start | bytes 16640 | tf_op jit(solution)/shard_map/ppermute | solution.py:27
  4.1 0.9 copy-start.3
  5.3 6.7 %collective-permute-start.2 = (bf16[77,3,128]{2,0,1:T(8,128)(2,1)S(1)}, bf16[77,3,128]{2,0,1:T(8,128)(2,1)S(1)}, u32[]{:S(2)}, u32[]{:S(2)}) collective-permute-start(bf16[77,3,128]{2,0,1:T(8,128)(2,1)S(1)} %get-tuple-element.22), channel_id=1, source_target_pairs={{0,2},{2,4},{4,6},{6,8},{8,10},{10,12},{12,14},{1,3},{3,5},{5,7},{... | collective-permute-start | bytes 177416 | tf_op jit(solution)/shard_map/ppermute | solution.py:27
  10.1 6.1 %collective-permute-start.3 = (bf16[77,3,128]{2,0,1:T(8,128)(2,1)S(1)}, bf16[77,3,128]{2,0,1:T(8,128)(2,1)S(1)}, u32[]{:S(2)}, u32[]{:S(2)}) collective-permute-start(bf16[77,3,128]{2,0,1:T(8,128)(2,1)S(1)} %get-tuple-element.23), channel_id=1, source_target_pairs={{2,0},{4,2},{6,4},{8,6},{10,8},{12,10},{14,12},{3,1},{5,3},{7,5},{... | collective-permute-start | bytes 177416 | tf_op jit(solution)/shard_map/ppermute | solution.py:27
  11.4 5.2 %copy-start = (bf16[77,256]{1,0:T(8,128)(2,1)S(1)}, bf16[77,256]{1,0:T(8,128)(2,1)}, u32[]{:S(2)}) copy-start(bf16[77,256]{1,0:T(8,128)(2,1)} %w_enc_ref.1) | copy-start | bytes 118276
  11.4 5.2 %copy-start.1 = (bf16[256,77]{0,1:T(8,128)(2,1)S(1)}, bf16[256,77]{0,1:T(8,128)(2,1)}, u32[]{:S(2)}) copy-start(bf16[256,77]{0,1:T(8,128)(2,1)} %param.17) | copy-start | bytes 118276
  16.6 0.7 copy-start.2
  100.7 1.1 %copy-start.4 = (bf16[1024,256]{1,0:T(8,128)(2,1)S(1)}, bf16[1024,256]{1,0:T(8,128)(2,1)}, u32[]{:S(2)}) copy-start(bf16[1024,256]{1,0:T(8,128)(2,1)} %get-tuple-element.20) | copy-start | bytes 1572868

commit v3 on v2

--- a/solution.py
+++ b/solution.py
@@ -287,19 +287,19 @@
         acc[base_enc : base_enc + chan, :] += dot(x_ref[r], g.astype(BF16), (1, 0))
 
     steps = groups * lane_parts
-    for piece in range(6):
-        pl.loop(piece * steps // 6, (piece + 1) * steps // 6)(depthwise_back)
+    for piece in range(3):
+        pl.loop(piece * steps // 3, (piece + 1) * steps // 3)(depthwise_back)
         next(flow, None)
-    for piece in range(2):
-        pl.loop(piece * wide // 2, (piece + 1) * wide // 2)(encoder_back)
-        next(flow, None)
+    pl.loop(0, wide)(encoder_back)
     for i in range(KSIZE * KSIZE):
         acc[base_dw + i : base_dw + i + 1, :] = jnp.sum(dk[i], axis=0, keepdims=True)
-    for _ in flow:
-        pass
-
     tail = exchange([2], False)
     next(tail)
+    for _ in range(bits + 1):
+        next(flow, None)
+        next(tail, None)
+    for _ in flow:
+        next(tail, None)
     small_out[...] = small_now[bits + 1]
     for k in range(hid // width):
         up_ref[:, k * width : (k + 1) * width] = res[k * width : (k + 1) * width, :]

time: 107 us -> 93.8 us (0.88)
  Pallas kernels: 81.6 us -> 68.5 us
    pallas_call x1, Pallas kernels: 81.6 us -> 68.5 us  [shards(): pl.pallas_call(functools.partial(block_kernel, ranges, band_size), out_sh...]
where the time goes in v3:
time: 93.8 us; the launch traced here: 93.5 us
  Pallas kernels  68.5 us (73%)
  starting transfers between devices  6.74 us (7%)
  other arithmetic  6.42 us (7%)
  waiting for transfers between devices  4.78 us (5%)
  local copies, waits for them, and re-layouts  3.75 us (4%)
  between operations  3.28 us (3%)
    pallas_call x1, Pallas kernels, shards(): pl.pallas_call(functools.partial(block_kernel, ranges, band_size), out_sh...  68.5 us
    ppermute x4, starting transfers between devices, with_halo(): return (lax.ppermute(last, axis, up), lax.ppermute(leading, axis, down))  6.74 us
    ppermute x4, waiting for transfers between devices, with_halo(): return (lax.ppermute(last, axis, up), lax.ppermute(leading, axis, down))  4.78 us
  transfers between devices with their start and end apart: 4, of which 2 were waited for; matrix products, arithmetic and copies ran while one was open for 1% of the time, Pallas kernels for 0%

profile of v3, /device:TPU:0, one launch (start us, length us, event | category | flops | bytes accessed | tf_op | source)
XLA Modules:
  0.0 93.5 jit_solution(16621348865047890213)
XLA Ops:
  0.7 1.2 %fusion.1 = (bf16[77,12,3]{2,0,1:T(8,128)(2,1)S(1)}, bf16[77,12,3]{2,0,1:T(8,128)(2,1)S(1)}) fusion(bf16[77,12,120]{2,0,1:T(8,128)(2,1)} %param.9), kind=kLoop, calls=%fused_computation.12 | loop fusion | bytes 22176 | tf_op jit(solution)/shard_map/slice | solution.py:25
  1.9 0.0 copy-start.6
  1.9 0.5 collective-permute-start
  2.4 0.1 collective-permute-start.1
  2.5 0.0 copy-done.7
  2.5 0.6 convert_reduce_fusion
  3.1 0.1 fusion
  3.2 0.1 broadcast_in_dim.9
  3.3 0.1 broadcast_in_dim.10
  4.1 0.1 pad.8.goal_ref
  4.1 0.0 copy-start.3
  4.1 0.0 collective-permute-done
  4.1 0.0 collective-permute-done.1
  4.2 0.9 copy-done.3
  5.1 0.2 pad_maximum_fusion.3
  5.3 4.9 %collective-permute-start.2 = (bf16[77,3,128]{2,0,1:T(8,128)(2,1)S(1)}, bf16[77,3,128]{2,0,1:T(8,128)(2,1)S(1)}, u32[]{:S(2)}, u32[]{:S(2)}) collective-permute-start(bf16[77,3,128]{2,0,1:T(8,128)(2,1)S(1)} %get-tuple-element.22), channel_id=1, source_target_pairs={{0,2},{2,4},{4,6},{6,8},{8,10},{10,12},{12,14},{1,3},{3,5},{5,7},{... | collective-permute-start | bytes 177416 | tf_op jit(solution)/shard_map/ppermute | solution.py:27
  10.1 1.3 %collective-permute-start.3 = (bf16[77,3,128]{2,0,1:T(8,128)(2,1)S(1)}, bf16[77,3,128]{2,0,1:T(8,128)(2,1)S(1)}, u32[]{:S(2)}, u32[]{:S(2)}) collective-permute-start(bf16[77,3,128]{2,0,1:T(8,128)(2,1)S(1)} %get-tuple-element.23), channel_id=1, source_target_pairs={{2,0},{4,2},{6,4},{8,6},{10,8},{12,10},{14,12},{3,1},{5,3},{7,5},{... | collective-permute-start | bytes 177416 | tf_op jit(solution)/shard_map/ppermute | solution.py:27
  11.4 0.0 copy-start
  11.4 0.0 copy-start.1
  11.5 0.5 collective-permute-done.2
  12.0 4.3 %collective-permute-done.3 = bf16[77,3,128]{2,0,1:T(8,128)(2,1)S(1)} collective-permute-done((bf16[77,3,128]{2,0,1:T(8,128)(2,1)S(1)}, bf16[77,3,128]{2,0,1:T(8,128)(2,1)S(1)}, u32[]{:S(2)}, u32[]{:S(2)}) %collective-permute-start.3) | collective-permute-done | bytes 59168 | tf_op jit(solution)/shard_map/ppermute | solution.py:27
  16.2 0.3 maximum_bitcast_fusion.x_ref
  16.6 0.0 copy-start.2
  16.6 0.7 copy-done.2
  17.3 68.5 %block.1 = (bf16[12,77,128]{2,1,0:T(8,128)(2,1)S(1)}, f32[8,256]{1,0:T(8,128)S(1)}, bf16[256,1024]{1,0:T(8,128)(2,1)S(1)}, bf16[1024,256]{1,0:T(8,128)(2,1)}, bf...) custom-call(bf16[18,77,128]{2,1,0:T(8,128)(2,1)S(1)} %maximum_bitcast_fusion.x_ref, ...), custom_call_target="tpu_custom_call" | custom-call | tf_op jit(solution)/shard_map/block/pallas_call | solution.py:345
  85.8 1.2 %fusion.2 = (f32[1,256]{1,0:T(1,128)}, f32[]{:T(128)}) fusion(f32[8,256]{1,0:T(8,128)S(1)} %get-tuple-element.16), kind=kLoop, calls=%fused_computation.13 | loop fusion | flops 255 | bytes 3076 | tf_op jit(solution)/shard_map/slice | solution.py:392
  87.6 1.1 %convert_element_type.39 = f32[256,1024]{1,0:T(8,128)} convert(bf16[256,1024]{1,0:T(8,128)(2,1)S(1)} %get-tuple-element.19) | non-fusion elementwise | flops 262144 | bytes 1572864 | tf_op jit(solution)/shard_map/convert_element_type | solution.py:393
  88.7 1.0 %convert_element_type.40 = f32[1024,256]{1,0:T(8,128)} convert(bf16[1024,256]{1,0:T(8,128)(2,1)S(1)} %copy-done.4) | non-fusion elementwise | flops 262144 | bytes 1572864 | tf_op jit(solution)/shard_map/convert_element_type | solution.py:394
  89.7 0.7 slice_bitcast_fusion
  90.5 0.6 convert_bitcast_fusion
  91.1 0.6 convert_element_type.37
  91.7 0.6 convert_element_type.38
  (11 shorter events, 0.1 us)
Async XLA Ops:
  0.6 1.9 %copy-start.7 = (s32[8,20]{1,0:T(8,128)S(1)}, s32[8,20]{1,0:T(8,128)}, u32[]{:S(2)}) copy-start(s32[8,20]{1,0:T(8,128)} %param.11) | copy-start | bytes 1924
  0.6 3.4 %copy-start.5 = (bf16[77,12,120]{2,0,1:T(8,128)(2,1)S(1)}, bf16[77,12,120]{2,0,1:T(8,128)(2,1)}, u32[]{:S(2)}) copy-start(bf16[77,12,120]{2,0,1:T(8,128)(2,1)} %param.10) | copy-start | bytes 665284
  1.9 1.4 %copy-start.6 = (bf16[49,256]{1,0:T(8,128)(2,1)S(1)}, bf16[49,256]{1,0:T(8,128)(2,1)}, u32[]{:S(2)}) copy-start(bf16[49,256]{1,0:T(8,128)(2,1)} %param.13) | copy-start | bytes 75268
  1.9 2.2 %collective-permute-start = (bf16[77,12,3]{2,0,1:T(8,128)(2,1)S(1)}, bf16[77,12,3]{2,0,1:T(8,128)(2,1)S(1)}, u32[]{:S(2)}, u32[]{:S(2)}) collective-permute-start(bf16[77,12,3]{2,0,1:T(8,128)(2,1)S(1)} %get-tuple-element.24), channel_id=1, source_target_pairs={{0,1},{1,0},{2,3},{3,2},{4,5},{5,4},{6,7},{7,6},{8,9},{9,8},{10,11... | collective-permute-start | bytes 16640 | tf_op jit(solution)/shard_map/ppermute | solution.py:27
  2.4 1.7 %collective-permute-start.1 = (bf16[77,12,3]{2,0,1:T(8,128)(2,1)S(1)}, bf16[77,12,3]{2,0,1:T(8,128)(2,1)S(1)}, u32[]{:S(2)}, u32[]{:S(2)}) collective-permute-start(bf16[77,12,3]{2,0,1:T(8,128)(2,1)S(1)} %get-tuple-element.25), channel_id=1, source_target_pairs={{1,0},{0,1},{3,2},{2,3},{5,4},{4,5},{7,6},{6,7},{9,8},{8,9},{11,10... | collective-permute-start | bytes 16640 | tf_op jit(solution)/shard_map/ppermute | solution.py:27
  4.1 0.9 %copy-start.3 = (bf16[77,12,120]{2,0,1:T(8,128)(2,1)S(1)}, bf16[77,12,120]{2,0,1:T(8,128)(2,1)}, u32[]{:S(2)}) copy-start(bf16[77,12,120]{2,0,1:T(8,128)(2,1)} %param.9) | copy-start | bytes 665284
  5.3 6.7 %collective-permute-start.2 = (bf16[77,3,128]{2,0,1:T(8,128)(2,1)S(1)}, bf16[77,3,128]{2,0,1:T(8,128)(2,1)S(1)}, u32[]{:S(2)}, u32[]{:S(2)}) collective-permute-start(bf16[77,3,128]{2,0,1:T(8,128)(2,1)S(1)} %get-tuple-element.22), channel_id=1, source_target_pairs={{0,2},{2,4},{4,6},{6,8},{8,10},{10,12},{12,14},{1,3},{3,5},{5,7},{... | collective-permute-start | bytes 177416 | tf_op jit(solution)/shard_map/ppermute | solution.py:27
  10.1 6.1 %collective-permute-start.3 = (bf16[77,3,128]{2,0,1:T(8,128)(2,1)S(1)}, bf16[77,3,128]{2,0,1:T(8,128)(2,1)S(1)}, u32[]{:S(2)}, u32[]{:S(2)}) collective-permute-start(bf16[77,3,128]{2,0,1:T(8,128)(2,1)S(1)} %get-tuple-element.23), channel_id=1, source_target_pairs={{2,0},{4,2},{6,4},{8,6},{10,8},{12,10},{14,12},{3,1},{5,3},{7,5},{... | collective-permute-start | bytes 177416 | tf_op jit(solution)/shard_map/ppermute | solution.py:27
  11.4 5.2 %copy-start = (bf16[77,256]{1,0:T(8,128)(2,1)S(1)}, bf16[77,256]{1,0:T(8,128)(2,1)}, u32[]{:S(2)}) copy-start(bf16[77,256]{1,0:T(8,128)(2,1)} %w_enc_ref.1) | copy-start | bytes 118276
  11.4 5.2 %copy-start.1 = (bf16[256,77]{0,1:T(8,128)(2,1)S(1)}, bf16[256,77]{0,1:T(8,128)(2,1)}, u32[]{:S(2)}) copy-start(bf16[256,77]{0,1:T(8,128)(2,1)} %param.17) | copy-start | bytes 118276
  16.6 0.7 copy-start.2
  87.6 1.1 %copy-start.4 = (bf16[1024,256]{1,0:T(8,128)(2,1)S(1)}, bf16[1024,256]{1,0:T(8,128)(2,1)}, u32[]{:S(2)}) copy-start(bf16[1024,256]{1,0:T(8,128)(2,1)} %get-tuple-element.20) | copy-start | bytes 1572868

commit v4 on v3

--- a/solution.py
+++ b/solution.py
@@ -18,15 +18,6 @@
 GELU_A = 0.044715
 
 
-def with_halo(value, axis, dim, width, wrap):
-    size, length = (lax.axis_size(axis), value.shape[dim])
-    up = [(i, (i + 1) % size) for i in range(size if wrap else size - 1)]
-    down = [(j, i) for i, j in up]
-    last = lax.slice_in_dim(value, length - width, length, axis=dim)
-    leading = lax.slice_in_dim(value, 0, width, axis=dim)
-    return lax.ppermute(last, axis, up), lax.ppermute(leading, axis, down)
-
-
 def dot(left, right, dims):
     return lax.dot_general(left, right, ((dims[:1], dims[1:]), ((), ())), preferred_element_type=F32)
 
@@ -39,9 +30,11 @@
     ranges, band_size, x_ref, goal_ref, mask_ref, gscale_ref, w_enc_ref, dw_ref, gain_ref, w_up_ref,
     w_down_ref, w_dec_t_ref, pred_ref, small_out, up_ref, down_ref, enc_ref, dw_out, dec_ref,
     shifted, conv, gres_all, taps, dk, up_acc, down_acc, acc, core_in, out_buf, in_buf, res,
-    small_now, small_in, send_sem, recv_sem, small_send, small_recv,
+    small_now, small_in, send_sem, recv_sem, small_send, small_recv, x_all, x_other, edge, halo_send,
+    halo_recv,
 ):
-    chan = x_ref.shape[1]
+    chan = w_dec_t_ref.shape[0]
+    deep = x_ref.shape[1]
     width = w_enc_ref.shape[1]
     hid = w_up_ref.shape[1]
     rows = goal_ref.shape[0]
@@ -67,6 +60,16 @@
     barrier = pltpu.get_barrier_semaphore()
     for peer in [core] + [across(bit) for bit in range(bits)]:
         pl.semaphore_signal(barrier, inc=1, device_id=peer, device_id_type=pl.DeviceIdType.MESH)
+
+    extra = band - 1 + 2 * digit(0)
+    has_extra = (extra >= 0) & (extra < band_size)
+
+    @pl.when(has_extra)
+    def _():
+        pl.semaphore_signal(
+            barrier, inc=1, device_id={"band": extra, "sub": sub},
+            device_id_type=pl.DeviceIdType.MESH,
+        )
 
     def send(src, dst, send_at, recv_at, peer):
         copy = pltpu.make_async_remote_copy(
@@ -176,12 +179,84 @@
     small_now[0] = jnp.zeros((8, width), F32)
     inside = lax.broadcasted_iota(jnp.int32, (LANES, width), 0) < groups * 8
 
-    @pl.loop(0, wide)
-    def _(r):
-        enc = dot(x_ref[r], w_enc_ref[...], (0, 0)).astype(BF16).astype(F32)
+    def northward():
+        return pltpu.make_async_remote_copy(
+            src_ref=x_ref.at[pl.ds(0, RIM)], dst_ref=edge.at[1],
+            send_sem=halo_send.at[1], recv_sem=halo_recv.at[1],
+            device_id={"band": (band + band_size - 1) % band_size, "sub": sub},
+            device_id_type=pl.DeviceIdType.MESH,
+        )
+
+    def southward():
+        return pltpu.make_async_remote_copy(
+            src_ref=x_ref.at[pl.ds(rows - RIM, RIM)], dst_ref=edge.at[0],
+            send_sem=halo_send.at[2], recv_sem=halo_recv.at[2],
+            device_id={"band": (band + 1) % band_size, "sub": sub},
+            device_id_type=pl.DeviceIdType.MESH,
+        )
+
+    has_north = band > 0
+    has_south = band < band_size - 1
+    pl.semaphore_wait(barrier, bits + 1 + has_extra.astype(jnp.int32))
+
+    strip = send(x_ref, x_other.at[pl.ds(RIM, rows)], halo_send.at[0], halo_recv.at[0], core)
+
+    @pl.when(has_north)
+    def _():
+        northward().start()
+
+    @pl.when(has_south)
+    def _():
+        southward().start()
+
+    lane = lax.broadcasted_iota(jnp.int32, (deep, LANES), 1)
+    span = groups * 8
+
+    def encode(own, other, r):
+        far = other.astype(F32)
+        left = pltpu.roll(far, LANES - span, 1)
+        right = pltpu.roll(far, span, 1)
+        near = jnp.where(lane < RIM, left, jnp.where(lane < span + RIM, own.astype(F32), right))
+        cells = jnp.where(lane < span + 2 * RIM, near, 0.0).astype(BF16)
+        x_all[r] = cells
+        enc = dot(cells, w_enc_ref[...], (0, 0)).astype(BF16).astype(F32)
         for b in range(KSIZE):
             moved = enc if b == 0 else pltpu.roll(enc, LANES - b, 0)
             shifted[b, r] = jnp.where(inside, moved, 0.0)
+
+    strip.wait_recv()
+
+    @pl.loop(0, rows)
+    def _(y):
+        encode(x_ref[y], x_other[y + RIM], y + RIM)
+
+    @pl.when(has_north)
+    def _():
+        southward().wait_recv()
+
+    @pl.when(band == 0)
+    def _():
+        edge[0] = jnp.zeros((RIM, deep, LANES), BF16)
+
+    @pl.when(has_south)
+    def _():
+        northward().wait_recv()
+
+    @pl.when(band == band_size - 1)
+    def _():
+        edge[1] = jnp.zeros((RIM, deep, LANES), BF16)
+
+    top = send(edge.at[0], x_other.at[pl.ds(0, RIM)], halo_send.at[3], halo_recv.at[3], core)
+    bottom = send(
+        edge.at[1], x_other.at[pl.ds(rows + RIM, RIM)], halo_send.at[4], halo_recv.at[4], core
+    )
+    top.wait_recv()
+    bottom.wait_recv()
+
+    @pl.loop(0, RIM)
+    def _(k):
+        encode(edge[0, k], x_other[k], k)
+        encode(edge[1, k], x_other[rows + RIM + k], rows + RIM + k)
 
     conv[:, groups * 8 :, :] = jnp.zeros((rows, LANES - groups * 8, width), F32)
 
@@ -224,7 +299,7 @@
         readout = dot(w_dec_t_ref[...], residual, (1, 1))
         base = jnp.concatenate(
             [
-                pltpu.roll(x_ref[y + RIM + i].astype(F32), LANES - RIM, 1)
+                pltpu.roll(x_all[y + RIM + i].astype(F32), LANES - RIM, 1)[:chan]
                 for i in range(2)
             ],
             axis=1,
@@ -258,7 +333,6 @@
         acc[cols, :] = up_acc[:, cols]
         acc[hid + k * width : hid + (k + 1) * width, :] = down_acc[:, cols].T
 
-    pl.semaphore_wait(barrier, bits + 1)
     flow = exchange([0, 1], True)
     next(flow)
 
@@ -284,7 +358,7 @@
         g = pltpu.roll(gres_all[r], RIM, 0) + shifted[0, r]
         for b in range(1, KSIZE):
             g = g + pltpu.roll(shifted[b, r], b, 0)
-        acc[base_enc : base_enc + chan, :] += dot(x_ref[r], g.astype(BF16), (1, 0))
+        acc[base_enc : base_enc + deep, :] += dot(x_all[r], g.astype(BF16), (1, 0))
 
     steps = groups * lane_parts
     for piece in range(3):
@@ -312,6 +386,14 @@
     for copy in started:
         copy.wait_send()
 
+    @pl.when(has_north)
+    def _():
+        northward().wait_send()
+
+    @pl.when(has_south)
+    def _():
+        southward().wait_send()
+
 
 def shards(state, target, tile_plan, w_enc, dw_kernel, norm_gain, w_up, w_down, w_dec):
     chan, rows, cols = state.shape
@@ -320,11 +402,11 @@
     tile_cols = cols // PW
     band_at = lax.axis_index("band")
     sub_at = lax.axis_index("sub")
-    before, after = with_halo(state, "sub", 2, RIM, True)
-    fill = jnp.zeros((chan, rows, LANES - cols - 2 * RIM), BF16)
-    lon = jnp.concatenate([before, state, after, fill], axis=2)
-    above, below = with_halo(lon, "band", 1, RIM, False)
-    x = jnp.concatenate([above, lon, below], axis=1).transpose(1, 0, 2)
+    deep = -(-chan // 16) * 16
+    x = jnp.pad(
+        state.transpose(1, 0, 2), ((0, 0), (0, deep - chan), (RIM, LANES - cols - RIM))
+    )
+    w_in = jnp.pad(w_enc, ((0, deep - chan), (0, 0)))
     goal = jnp.pad(target.transpose(1, 0, 2), ((0, 0), (0, 0), (0, LANES - cols)))
     plan = lax.dynamic_slice(tile_plan, (band_at, sub_at * tile_cols), (1, tile_cols))
     wet = (plan >= 0).astype(F32)
@@ -374,13 +456,18 @@
             dma((3, 2 * bits + 2)),
             dma((bits + 1,)),
             dma((bits + 1,)),
+            pltpu.VMEM((wide, deep, LANES), BF16),
+            pltpu.VMEM((wide, deep, LANES), BF16),
+            pltpu.VMEM((2, RIM, deep, LANES), BF16),
+            dma((5,)),
+            dma((5,)),
         ],
         compiler_params=pltpu.CompilerParams(
             collective_id=0, has_side_effects=True, vmem_limit_bytes=52 * 1024 * 1024
         ),
         name="block",
     )(
-        x, goal, mask, mask * (2.0 * inv_count), w_enc, dw_kernel.astype(F32),
+        x, goal, mask, mask * (2.0 * inv_count), w_in, dw_kernel.astype(F32),
         norm_gain.reshape(1, width), w_up, w_down, w_dec.T,
     )
     new_field = pred[:, :, :cols].transpose(1, 0, 2)

time: 93.8 us -> 90.1 us (0.961)
  Pallas kernels: 68.5 us -> 75.6 us
  starting transfers between devices: 6.74 us -> 0 us
  waiting for transfers between devices: 4.78 us -> 0 us
  local copies, waits for them, and re-layouts: 3.75 us -> 4.95 us
    pallas_call x1, Pallas kernels: 68.5 us -> 75.6 us  [shards(): pl.pallas_call(functools.partial(block_kernel, ranges, band_size), out_sh...]
    ppermute x4 -> x0, starting transfers between devices: 6.74 us -> none  [with_halo(): return (lax.ppermute(last, axis, up), lax.ppermute(leading, axis, down))]
    ppermute x4 -> x0, waiting for transfers between devices: 4.78 us -> none  [with_halo(): return (lax.ppermute(last, axis, up), lax.ppermute(leading, axis, down))]
    unnamed x16 -> x14, local copies, waits for them, and re-layouts: 1.56 us -> 2.9 us
    slice x1 -> x0, local copies, waits for them, and re-layouts: 1.24 us -> none  [with_halo(): last = lax.slice_in_dim(value, length - width, length, axis=dim)]
    pad x0 -> x2, local copies, waits for them, and re-layouts: none -> 1.13 us  [the longest x1 1.12 us: shards(): jnp.pad(state.transpose(1, 0, 2), ((0, 0), (0, deep - chan), (RIM, LANES...]
  transfers between devices with their start and end apart: 4 -> 0, of which waited for: 2 -> 0; matrix products, arithmetic and copies ran while one was open for 1% -> 0% of each run, Pallas kernels for 0% -> 0%
where the time goes in v4:
time: 90.1 us; the launch traced here: 89.7 us
  Pallas kernels  75.6 us (84%)
  other arithmetic  5.9 us (7%)
  local copies, waits for them, and re-layouts  4.95 us (5%)
  between operations  3.2 us (4%)
    pallas_call x1, Pallas kernels, shards(): pl.pallas_call(functools.partial(block_kernel, ranges, band_size), out_sh...  75.6 us
    unnamed x14, local copies, waits for them, and re-layouts  2.9 us

profile of v4, /device:TPU:0, one launch (start us, length us, event | category | flops | bytes accessed | tf_op | source)
XLA Modules:
  0.0 89.7 jit_solution(14674714037653547677)
XLA Ops:
  0.6 0.0 copy-start.6
  0.6 0.7 copy-done.6
  1.3 0.1 fusion
  1.4 0.1 broadcast_in_dim.5
  1.5 0.1 broadcast_in_dim.6
  1.6 0.6 convert_reduce_fusion
  2.9 0.0 copy-start.3
  2.9 1.1 %pad.16.x_ref = bf16[12,80,128]{2,1,0:T(8,128)(2,1)S(1)} pad(bf16[12,77,120]{2,1,0:T(8,128)(2,1)} %bitcast.14, bf16[]{:T(256)} %constant.11.clone.1), padding=0_0x0_3x3_5 | pad | bytes 467522 | tf_op jit(solution)/shard_map/jit(_pad)/pad | solution.py:406
  4.0 0.0 copy-done.3
  4.0 0.0 copy-start.5
  4.0 0.1 pad.17.goal_ref
  4.1 0.7 copy-done.5
  4.8 0.0 copy-start.4
  4.8 0.8 copy-done.4
  5.5 0.0 copy-start
  5.6 0.0 copy-start.1
  5.6 0.8 copy-done
  6.3 0.0 copy-done.1
  6.3 75.6 %block.1 = (bf16[12,77,128]{2,1,0:T(8,128)(2,1)S(1)}, f32[8,256]{1,0:T(8,128)S(1)}, bf16[256,1024]{1,0:T(8,128)(2,1)S(1)}, bf16[1024,256]{1,0:T(8,128)(2,1)}, bf...) custom-call(bf16[12,80,128]{2,1,0:T(8,128)(2,1)S(1)} %pad.16.x_ref, ...), custom_call_target="tpu_custom_call" | custom-call | tf_op jit(solution)/shard_map/block/pallas_call | solution.py:427
  82.0 1.2 %fusion.1 = (f32[1,256]{1,0:T(1,128)}, f32[]{:T(128)}) fusion(f32[8,256]{1,0:T(8,128)S(1)} %get-tuple-element.16), kind=kLoop, calls=%fused_computation.7 | loop fusion | flops 255 | bytes 3076 | tf_op jit(solution)/shard_map/slice | solution.py:479
  83.8 0.0 copy-start.2
  83.8 1.1 %convert_element_type.43 = f32[256,1024]{1,0:T(8,128)} convert(bf16[256,1024]{1,0:T(8,128)(2,1)S(1)} %get-tuple-element.19) | non-fusion elementwise | flops 262144 | bytes 1572864 | tf_op jit(solution)/shard_map/convert_element_type | solution.py:480
  84.9 0.0 copy-done.2
  84.9 1.0 %convert_element_type.44 = f32[1024,256]{1,0:T(8,128)} convert(bf16[1024,256]{1,0:T(8,128)(2,1)S(1)} %copy-done.2) | non-fusion elementwise | flops 262144 | bytes 1572864 | tf_op jit(solution)/shard_map/convert_element_type | solution.py:481
  85.9 0.7 slice_bitcast_fusion
  86.6 0.6 convert_bitcast_fusion
  87.3 0.6 convert_element_type.41
  87.9 0.6 convert_element_type.42
  (3 shorter events, 0.0 us)
Async XLA Ops:
  0.6 0.7 copy-start.6
  2.9 1.1 %copy-start.3 = (bf16[77,12,120]{2,0,1:T(8,128)(2,1)S(1)}, bf16[77,12,120]{2,0,1:T(8,128)(2,1)}, u32[]{:S(2)}) copy-start(bf16[77,12,120]{2,0,1:T(8,128)(2,1)} %param.10) | copy-start | bytes 665284
  4.0 0.8 copy-start.5
  4.8 0.8 copy-start.4
  5.5 0.8 copy-start
  5.6 0.8 copy-start.1
  83.8 1.1 %copy-start.2 = (bf16[1024,256]{1,0:T(8,128)(2,1)S(1)}, bf16[1024,256]{1,0:T(8,128)(2,1)}, u32[]{:S(2)}) copy-start(bf16[1024,256]{1,0:T(8,128)(2,1)} %get-tuple-element.20) | copy-start | bytes 1572868
